TPU v7x, 128 devices: a whole 4x4x4 slice. The times are simulated.
128 devices in a mesh: rows: 32 (over x, z_hi, y), ch: 4 (over z_lo, core).
Axes of the slice: x: 4, y: 4, z: 4 (z_hi: 2, z_lo: 2; z = z_hi * 2 + z_lo), core: 2. Of those that a mesh axis runs over, the one named last changes fastest.
Arguments:
- pair: bfloat16 [128, 512, 512], P('ch', 'rows'), may hold values from -6 to 6
- residue_mask: int32 [512], replicated, may hold values 0 or 1
- chain_ids: int32 [512], replicated, may hold values from 0 to 3, never falling along the last dimension, each value on 1 to 256 neighbouring positions
- pair_gain: float32 [2, 128], replicated, may hold values from 0.1 to 1.9
- pair_bias: float32 [2, 128], replicated, may hold values from -3 to 3
- in_weight: bfloat16 [2, 4, 128, 128], P(None, None, None, 'ch'), may hold values from -0.5 to 0.5
- gate_weight: bfloat16 [2, 128, 128], P(None, None, 'ch'), may hold values from -0.5 to 0.5
- hidden_gain: float32 [2, 128], P(None, 'ch'), may hold values from 0.1 to 1.9
- hidden_bias: float32 [2, 128], P(None, 'ch'), may hold values from -3 to 3
- cross_gain: float32 [2, 128], P(None, 'ch'), may hold values from 0.3 to 1.7
- out_weight: bfloat16 [2, 128, 128], replicated, may hold values from -0.5 to 0.5
Outputs:
- pair_out: bfloat16 [128, 512, 512], P('ch', 'rows')
All inputs are finite; a program needn't handle non-finite values.
Results may differ from a plain program's by a relative error of at most 0.014.
Values may be sent and summed in bfloat16 or wider, within the bound.
A program may use at most 192 MiB of HBM per device.

v0:
```python
import jax
import jax.numpy as jnp
from jax import lax
from jax.sharding import PartitionSpec as P

C = 128
HID = 128


def norm_local(values, gain, offset, width, site_kind):
    totals = jnp.sum(values, axis=0)
    squares = jnp.sum(values * values, axis=0)
    if site_kind == 0:
        totals, squares = lax.psum((totals, squares), "ch")
    else:
        totals, squares = lax.psum((totals, squares), "ch")
    center = totals / width
    spread = squares / width - center * center
    return (
        (values - center) * lax.rsqrt(spread + 1e-05) * gain[:, None, None] + offset[:, None, None]
    ).astype(jnp.bfloat16)


def apply_update(
    current,
    layer,
    factor_rows,
    pair_gain,
    pair_bias,
    in_weight,
    gate_weight,
    hidden_gain,
    hidden_bias,
    cross_gain,
    out_weight,
):
    chan_local = current.shape[0]
    chan_index = lax.axis_index("ch")
    pair_f = current.astype(jnp.float32)
    gain_part = lax.dynamic_slice_in_dim(pair_gain[layer], chan_index * chan_local, chan_local, 0)
    bias_part = lax.dynamic_slice_in_dim(pair_bias[layer], chan_index * chan_local, chan_local, 0)
    normed_local = norm_local(pair_f, gain_part, bias_part, C, 0)
    normed = lax.all_gather(normed_local, "ch", axis=0, tiled=True)
    proj = jnp.einsum("pch,cij->phij", in_weight[layer], normed, preferred_element_type=jnp.float32)
    factor = factor_rows[0][None] * jnp.where(
        factor_rows[1][None] > 0.5, cross_gain[layer][:, None, None], 1.0
    )
    left = (factor * jax.nn.sigmoid(proj[0]) * proj[1]).astype(jnp.bfloat16)
    right = (factor * jax.nn.sigmoid(proj[2]) * proj[3]).astype(jnp.bfloat16)
    hidden_local = left.shape[0]
    if layer == 0:
        tri = jnp.einsum(
            "hik,hjk->hij",
            left,
            lax.all_gather(right, "rows", axis=1, tiled=True),
            preferred_element_type=jnp.float32,
        )
    else:
        left_cols = lax.all_to_all(left, "rows", split_axis=2, concat_axis=1, tiled=True)
        tri = jnp.einsum(
            "hki,hkj->hij",
            left_cols,
            lax.all_gather(right, "rows", axis=1, tiled=True),
            preferred_element_type=jnp.float32,
        )
    tri_normed = norm_local(tri, hidden_gain[layer], hidden_bias[layer], HID, 1)
    gate = jax.nn.sigmoid(
        jnp.einsum("cd,cij->dij", gate_weight[layer], normed, preferred_element_type=jnp.float32)
    )
    weight_rows = lax.dynamic_slice_in_dim(
        out_weight[layer], chan_index * hidden_local, hidden_local, 0
    )
    update = lax.psum_scatter(
        jnp.einsum("hd,hij->dij", weight_rows, tri_normed, preferred_element_type=jnp.float32),
        "ch",
        scatter_dimension=0,
        tiled=True,
    )
    return (pair_f + gate * update).astype(jnp.bfloat16)


def per_device(
    pair,
    residue_mask,
    chain_ids,
    pair_gain,
    pair_bias,
    in_weight,
    gate_weight,
    hidden_gain,
    hidden_bias,
    cross_gain,
    out_weight,
):
    local_rows = pair.shape[1]
    first_row = lax.axis_index("rows") * local_rows
    mask_all = residue_mask.astype(jnp.float32)
    mask_rows = lax.dynamic_slice_in_dim(mask_all, first_row, local_rows)
    chain_rows = lax.dynamic_slice_in_dim(chain_ids, first_row, local_rows)
    pair_mask = mask_rows[:, None] * mask_all[None, :]
    crossing = jnp.where(chain_rows[:, None] != chain_ids[None, :], 1.0, 0.0)
    factor_rows = jnp.stack([pair_mask, crossing])
    current = pair
    for layer in range(2):
        current = apply_update(
            current,
            layer,
            factor_rows,
            pair_gain,
            pair_bias,
            in_weight,
            gate_weight,
            hidden_gain,
            hidden_bias,
            cross_gain,
            out_weight,
        )
    return current


def solution(mesh):
    placed = (
        P("ch", "rows", None),
        P(),
        P(),
        P(),
        P(),
        P(None, None, None, "ch"),
        P(None, None, "ch"),
        P(None, "ch"),
        P(None, "ch"),
        P(None, "ch"),
        P(),
    )
    return jax.shard_map(
        per_device, mesh=mesh, in_specs=placed, out_specs=P("ch", "rows", None), check_vma=False
    )
```

profile of v0, /device:TPU:1, one launch (start us, length us, event | category | flops | bytes accessed | tf_op | source)
XLA Modules:
  0.0 705.7 jit_solution(5422204213874091334)
XLA Ops:
  6.5 2.1 convert_reduce_fusion.1
  10.3 38.6 %all-reduce.15.cloned.1.call-done = (f32[16,512]{1,0:T(8,128)}, f32[16,512]{1,0:T(8,128)}) async-done(((f32[16,512]{1,0:T(8,128)}, f32[16,512]{1,0:T(8,128)}), (f32[16,512]{1,0:T(8,128)}, f32[16,512]{1,0:T(8,128)})) %all-reduce.15.cloned.1.call-update) | async-done | bytes 65552 | tf_op jit(solution)/shard_map/psum | solution.py:14
  49.7 2.2 fusion.21
  55.1 27.1 %all-gather.5.cloned.1.call-done = bf16[128,16,512]{2,0,1:T(8,128)(2,1)} async-done(((bf16[32,16,512]{2,0,1:T(8,128)(2,1)}), bf16[128,16,512]{2,0,1:T(8,128)(2,1)}) %all-gather.5.cloned.1.call-update) | async-done | bytes 2097168 | tf_op jit(solution)/shard_map/all_gather | solution.py:43
  82.2 2.4 convolution_bitcast_fusion.1
  86.2 156.7 %all-gather.7.cloned.1.call-done = bf16[32,512,512]{2,0,1:T(8,128)(2,1)} async-done(((bf16[32,16,512]{2,0,1:T(8,128)(2,1)}), bf16[32,512,512]{2,0,1:T(8,128)(2,1)}) %all-gather.7.cloned.1.call-update) | async-done | bytes 16777232 | tf_op jit(solution)/shard_map/all_gather | solution.py:55
  242.9 30.2 %fusion.82 = (f32[16,512]{1,0:T(8,128)}, f32[16,512]{1,0:T(8,128)}, f32[32,16,512]{2,1,0:T(8,128)S(1)}) fusion(bf16[32,512,512]{2,0,1:T(8,128)(2,1)} %all-gather.7.cloned.1.call-done, bf16[32,16,512]{2,0,1:T(8,128)(2,1)S(1)} %get-tuple-element.23), kind=kOutput, calls=%fused_computation.128 | convolution fusion | flops 269205504 | bytes 18415616 | tf_op jit(solution)/shard_map/hik,hjk->hij/dot_general | solution.py:52
  273.1 34.0 %all-reduce.13.cloned.1.call-done = (f32[16,512]{1,0:T(8,128)}, f32[16,512]{1,0:T(8,128)}) async-done(((f32[16,512]{1,0:T(8,128)}, f32[16,512]{1,0:T(8,128)}), (f32[16,512]{1,0:T(8,128)}, f32[16,512]{1,0:T(8,128)})) %all-reduce.13.cloned.1.call-update) | async-done | bytes 65552 | tf_op jit(solution)/shard_map/psum | solution.py:16
  308.2 2.7 fusion.60
  311.0 46.3 %reduce-scatter.3.cloned.1.call-done = f32[32,16,512]{2,0,1:T(8,128)} async-done(((f32[128,16,512]{2,0,1:T(8,128)}), f32[32,16,512]{2,0,1:T(8,128)}) %reduce-scatter.3.cloned.1.call-update) | async-done | bytes 1048592 | tf_op jit(solution)/shard_map/reduce_scatter | solution.py:73
  357.2 2.9 convert_reduce_fusion
  360.3 36.5 %all-reduce.11.cloned.1.call-done = (f32[16,512]{1,0:T(8,128)}, f32[16,512]{1,0:T(8,128)}) async-done(((f32[16,512]{1,0:T(8,128)}, f32[16,512]{1,0:T(8,128)}), (f32[16,512]{1,0:T(8,128)}, f32[16,512]{1,0:T(8,128)})) %all-reduce.11.cloned.1.call-update) | async-done | bytes 65552 | tf_op jit(solution)/shard_map/psum | solution.py:14
  398.7 30.2 %all-gather.9.cloned.1.call-done = bf16[128,16,512]{2,0,1:T(8,128)(2,1)} async-done(((bf16[32,16,512]{2,0,1:T(8,128)(2,1)}), bf16[128,16,512]{2,0,1:T(8,128)(2,1)}) %all-gather.9.cloned.1.call-update) | async-done | bytes 2097168 | tf_op jit(solution)/shard_map/all_gather | solution.py:43
  428.9 2.3 convolution_bitcast_fusion
  432.8 2.0 copy.46
  434.8 2.0 reshape.117
  436.8 23.3 %all_to_all.18 = bf16[32,2,4096]{2,1,0:T(2,128)(2,1)S(1)} all-to-all(bf16[32,2,4096]{2,1,0:T(2,128)(2,1)S(1)} %reshape.117), channel_id=1, replica_groups=mesh['rows'=32,'ch'=4] {'rows'}, dimensions={0} | all-to-all | bytes 1048576 | tf_op jit(solution)/shard_map/all_to_all | solution.py:59
  461.1 1.8 copy.48
  462.9 3.0 copy.49
  466.0 128.7 %all-gather.11.cloned.1.call-done = bf16[32,512,512]{2,0,1:T(8,128)(2,1)} async-done(((bf16[32,16,512]{2,0,1:T(8,128)(2,1)}), bf16[32,512,512]{2,0,1:T(8,128)(2,1)}) %all-gather.11.cloned.1.call-update) | async-done | bytes 16777232 | tf_op jit(solution)/shard_map/all_gather | solution.py:63
  594.6 17.2 %fusion.81 = (f32[16,512]{1,0:T(8,128)}, f32[16,512]{1,0:T(8,128)}, f32[32,16,512]{2,1,0:T(8,128)S(1)}) fusion(bf16[32,512,16]{1,2,0:T(8,128)(2,1)S(1)} %copy.49, bf16[32,512,512]{2,0,1:T(8,128)(2,1)} %all-gather.11.cloned.1.call-done), kind=kOutput, calls=%fused_computation.127 | convolution fusion | flops 269205504 | bytes 18415616 | tf_op jit(solution)/shard_map/hki,hkj->hij/dot_general | solution.py:60
  611.9 34.0 %all-reduce.9.cloned.1.call-done = (f32[16,512]{1,0:T(8,128)}, f32[16,512]{1,0:T(8,128)}) async-done(((f32[16,512]{1,0:T(8,128)}, f32[16,512]{1,0:T(8,128)}), (f32[16,512]{1,0:T(8,128)}, f32[16,512]{1,0:T(8,128)})) %all-reduce.9.cloned.1.call-update) | async-done | bytes 65552 | tf_op jit(solution)/shard_map/psum | solution.py:16
  647.0 2.7 fusion.58
  649.7 46.3 %reduce-scatter.5.cloned.1.call-done = f32[32,16,512]{2,0,1:T(8,128)} async-done(((f32[128,16,512]{2,0,1:T(8,128)}), f32[32,16,512]{2,0,1:T(8,128)}) %reduce-scatter.5.cloned.1.call-update) | async-done | bytes 1048592 | tf_op jit(solution)/shard_map/reduce_scatter | solution.py:73
  (64 shorter events, 16.8 us)
Async XLA Ops:
  6.5 42.4 %all-reduce.15.cloned.1.call-start = ((), (), s32[]{:S(2)}) async-start(), calls=%async_computation.12 | async-start | bytes 131072 | tf_op jit(solution)/shard_map/psum | solution.py:14
  8.7 73.6 %all-gather.5.cloned.1.call-start = ((), (), s32[]{:S(2)}) async-start(), calls=%async_computation.3 | async-start | bytes 2621440 | tf_op jit(solution)/shard_map/all_gather | solution.py:43
  52.0 190.9 %all-gather.7.cloned.1.call-start = ((), (), s32[]{:S(2)}) async-start(), calls=%async_computation.4 | async-start | bytes 17301504 | tf_op jit(solution)/shard_map/all_gather | solution.py:55
  84.6 1.6 copy-start.6
  86.1 221.0 %all-reduce.13.cloned.1.call-start = ((), (), s32[]{:S(2)}) async-start(), calls=%async_computation.11 | async-start | bytes 131072 | tf_op jit(solution)/shard_map/psum | solution.py:16
  242.9 30.2 %copy-start.7 = (f32[2,32]{1,0:T(2,128)S(1)}, f32[2,32]{1,0:T(2,128)}, u32[]{:S(2)}) copy-start(f32[2,32]{1,0:T(2,128)} %param.19) | copy-start | bytes 772
  242.9 30.2 %copy-start.8 = (f32[2,32]{1,0:T(2,128)S(1)}, f32[2,32]{1,0:T(2,128)}, u32[]{:S(2)}) copy-start(f32[2,32]{1,0:T(2,128)} %param.18) | copy-start | bytes 772
  273.1 84.2 %reduce-scatter.3.cloned.1.call-start = ((), (), s32[]{:S(2)}) async-start(), calls=%async_computation.5 | async-start | bytes 5242880 | tf_op jit(solution)/shard_map/reduce_scatter | solution.py:73
  308.2 49.1 %copy-start = (bf16[128,16,512]{2,0,1:T(8,128)(2,1)S(1)}, bf16[128,16,512]{2,0,1:T(8,128)(2,1)}, u32[]{:S(2)}) copy-start(bf16[128,16,512]{2,0,1:T(8,128)(2,1)} %all-gather.5.cloned.1.call-done) | copy-start | bytes 6291460
  308.2 49.1 %copy-start.2 = (bf16[32,16,512]{2,1,0:T(8,128)(2,1)S(1)}, bf16[32,16,512]{2,1,0:T(8,128)(2,1)}, u32[]{:S(2)}) copy-start(bf16[32,16,512]{2,1,0:T(8,128)(2,1)} %param.11) | copy-start | bytes 1572868
  308.2 49.0 %copy-start.9 = (bf16[2,128,32]{1,2,0:T(8,128)(2,1)S(1)}, bf16[2,128,32]{1,2,0:T(8,128)(2,1)}, u32[]{:S(2)}) copy-start(bf16[2,128,32]{1,2,0:T(8,128)(2,1)} %param.17) | copy-start | bytes 49156
  310.9 118.0 %copy-start.5 = (bf16[2,4,128,32]{2,3,1,0:T(8,128)(2,1)S(1)}, bf16[2,4,128,32]{2,3,1,0:T(8,128)(2,1)}, u32[]{:S(2)}) copy-start(bf16[2,4,128,32]{2,3,1,0:T(8,128)(2,1)} %param.16) | copy-start | bytes 196612
  310.9 85.9 %all-reduce.11.cloned.1.call-start = ((), (), s32[]{:S(2)}) async-start(), calls=%async_computation.10 | async-start | bytes 131072 | tf_op jit(solution)/shard_map/psum | solution.py:14
  360.1 72.6 %copy-start.3 = (bf16[32,16,512]{2,0,1:T(8,128)(2,1)}, bf16[32,16,512]{2,0,1:T(8,128)(2,1)S(1)}, u32[]{:S(2)}) copy-start(bf16[32,16,512]{2,0,1:T(8,128)(2,1)S(1)} %get-tuple-element.46) | copy-start | bytes 1572868
  360.1 68.7 %all-gather.9.cloned.1.call-start = ((), (), s32[]{:S(2)}) async-start(), calls=%async_computation.6 | async-start | bytes 2621440 | tf_op jit(solution)/shard_map/all_gather | solution.py:43
  398.6 196.0 %all-gather.11.cloned.1.call-start = ((), (), s32[]{:S(2)}) async-start(), calls=%async_computation.7 | async-start | bytes 17301504 | tf_op jit(solution)/shard_map/all_gather | solution.py:63
  432.8 213.2 %all-reduce.9.cloned.1.call-start = ((), (), s32[]{:S(2)}) async-start(), calls=%async_computation.9 | async-start | bytes 131072 | tf_op jit(solution)/shard_map/psum | solution.py:16
  611.9 84.2 %reduce-scatter.5.cloned.1.call-start = ((), (), s32[]{:S(2)}) async-start(), calls=%async_computation.8 | async-start | bytes 5242880 | tf_op jit(solution)/shard_map/reduce_scatter | solution.py:73
  647.0 49.1 %copy-start.1 = (bf16[128,16,512]{2,0,1:T(8,128)(2,1)S(1)}, bf16[128,16,512]{2,0,1:T(8,128)(2,1)}, u32[]{:S(2)}) copy-start(bf16[128,16,512]{2,0,1:T(8,128)(2,1)} %all-gather.9.cloned.1.call-done) | copy-start | bytes 6291460
  647.0 49.1 %copy-start.4 = (bf16[32,16,512]{2,0,1:T(8,128)(2,1)S(1)}, bf16[32,16,512]{2,0,1:T(8,128)(2,1)}, u32[]{:S(2)}) copy-start(bf16[32,16,512]{2,0,1:T(8,128)(2,1)} %copy-done.3) | copy-start | bytes 1572868
Sparse Core Ops, SparseCore 0:
  9.9 39.0 all-reduce.14
  52.1 30.0 all-gather.4
  86.2 156.5 all-gather.6
  273.2 33.9 all-reduce.12
  311.0 46.1 reduce-scatter.2
  360.3 36.5 all-reduce.10
  398.8 30.0 all-gather.8
  432.9 161.7 all-gather.10
  612.0 33.9 all-reduce.8
  649.8 46.1 reduce-scatter.4
where the time goes:
time: 706 us
  waiting for transfers between devices  579 us (82%)
  matrix products  62 us (9%)
  blocking collectives  23.3 us (3%)
  local copies, waits for them, and re-layouts  14.3 us (2%)
  between operations  13.7 us (2%)
  other arithmetic  13.5 us (2%)
    all_gather x2, waiting for transfers between devices, apply_update(): lax.all_gather(right, 'rows', axis=1, tiled=True)  285 us
    psum x4, waiting for transfers between devices, norm_local(): totals, squares = lax.psum((totals, squares), 'ch')  143 us
    reduce_scatter x2, waiting for transfers between devices, apply_update(): lax.psum_scatter(jnp.einsum('hd,hij->dij', weight_rows, tri_normed, prefe...  92.6 us
    all_gather x2, waiting for transfers between devices, apply_update(): normed = lax.all_gather(normed_local, 'ch', axis=0, tiled=True)  57.3 us
    dot_general x1, matrix products, apply_update(): jnp.einsum('hik,hjk->hij', left, lax.all_gather(right, 'rows', axis=1, ti...  30.2 us
    all_to_all x1, blocking collectives, apply_update(): lax.all_to_all(left, 'rows', split_axis=2, concat_axis=1, tiled=True)  23.3 us
    dot_general x1, matrix products, apply_update(): jnp.einsum('hki,hkj->hij', left_cols, lax.all_gather(right, 'rows', axis=...  17.2 us
  transfers between devices with their start and end apart: 10, of which 10 were waited for; matrix products, arithmetic and copies ran while one was open for 2% of the time, Pallas kernels for 0%

commit v1 on v0

v1 whole, which is shorter than its diff:
```python
import functools

import jax
import jax.numpy as jnp
from jax import lax
from jax.experimental import pallas as pl
from jax.experimental.pallas import tpu as pltpu
from jax.sharding import PartitionSpec as P

C = 128
HID = 128
N = 512
MESH = pl.DeviceIdType.MESH
VM = pl.BlockSpec(memory_space=pltpu.VMEM)
LIMIT = 48 * 2**20


def greet(partners):
    barrier = pltpu.get_barrier_semaphore()
    for dev in partners:
        pl.semaphore_signal(barrier, inc=1, device_id=dev, device_id_type=MESH)
    pl.semaphore_wait(barrier, len(partners))


def gather_kernel(pair, win, wgate, small, pair_all, win_all, wgate_all, small_all, send, recv, local):
    r = lax.axis_index("rows")
    c = lax.axis_index("ch")
    greet([(r, lax.rem(c + s, 4)) for s in (1, 2, 3)])

    def moves(dst):
        return [
            (pair.at[:, :, pl.ds(pl.multiple_of(dst * 128, 128), 128)], pair_all.at[pl.ds(c * 32, 32)]),
            (win, win_all.at[:, pl.ds(pl.multiple_of(c * 32, 32), 32)]),
            (wgate, wgate_all.at[:, pl.ds(pl.multiple_of(c * 32, 32), 32)]),
            (small, small_all.at[c]),
        ]

    copies = []
    for s in (1, 2, 3):
        dst = lax.rem(c + s, 4)
        for k, (a, b) in enumerate(moves(dst)):
            cp = pltpu.make_async_remote_copy(
                src_ref=a, dst_ref=b, send_sem=send.at[s - 1, k], recv_sem=recv.at[s - 1, k],
                device_id=(r, dst), device_id_type=MESH,
            )
            cp.start()
            copies.append(cp)
    own = [pltpu.make_async_copy(a, b, local.at[k]) for k, (a, b) in enumerate(moves(c))]
    for cp in own:
        cp.start()
    for cp in own + copies:
        cp.wait()


def scatter_kernel(cur, out, send, recv, local):
    r = lax.axis_index("rows")
    c = lax.axis_index("ch")
    greet([(r, lax.rem(c + s, 4)) for s in (1, 2, 3)])
    here = out.at[:, :, pl.ds(pl.multiple_of(c * 128, 128), 128)]
    copies = []
    for s in (1, 2, 3):
        dst = lax.rem(c + s, 4)
        cp = pltpu.make_async_remote_copy(
            src_ref=cur.at[pl.ds(dst * 32, 32)], dst_ref=here, send_sem=send.at[s - 1], recv_sem=recv.at[s - 1],
            device_id=(r, dst), device_id_type=MESH,
        )
        cp.start()
        copies.append(cp)
    own = pltpu.make_async_copy(cur.at[pl.ds(c * 32, 32)], here, local)
    own.start()
    own.wait()
    for cp in copies:
        cp.wait()


def swap_kernel(x, y, send, recv, local):
    me = lax.axis_index("rows") * 4 + lax.axis_index("ch")
    barrier = pltpu.get_barrier_semaphore()

    def place(s):
        d = lax.rem(me + s, 128)
        return d, (lax.div(d, 4), lax.rem(d, 4))

    @pl.loop(1, 128)
    def _(s):
        pl.semaphore_signal(barrier, inc=1, device_id=place(s)[1], device_id_type=MESH)

    pl.semaphore_wait(barrier, 127)

    @pl.loop(1, 128)
    def _(s):
        d, dev = place(s)
        pltpu.make_async_remote_copy(
            src_ref=x.at[d], dst_ref=y.at[me], send_sem=send, recv_sem=recv, device_id=dev, device_id_type=MESH
        ).start()

    own = pltpu.make_async_copy(x.at[me], y.at[me], local)
    own.start()
    own.wait()
    whole = pltpu.make_async_remote_copy(
        src_ref=x.at[pl.ds(0, 127)], dst_ref=y.at[pl.ds(0, 127)], send_sem=send, recv_sem=recv,
        device_id=place(1)[1], device_id_type=MESH,
    )
    whole.wait_recv()
    whole.wait_send()


def gather(*args):
    dma = pltpu.SemaphoreType.DMA
    shape = jax.ShapeDtypeStruct
    return pl.pallas_call(
        gather_kernel,
        out_shape=(
            shape((C, 16, 128), jnp.bfloat16), shape((8, 128, 128), jnp.bfloat16),
            shape((2, 128, 128), jnp.bfloat16), shape((4, 8, 128), jnp.float32),
        ),
        in_specs=[VM] * 4, out_specs=(VM,) * 4,
        scratch_shapes=[dma((3, 4)), dma((3, 4)), dma((4,))],
        compiler_params=pltpu.CompilerParams(collective_id=0, has_side_effects=True, vmem_limit_bytes=LIMIT),
    )(*args)


def scatter(cur):
    dma = pltpu.SemaphoreType.DMA
    return pl.pallas_call(
        scatter_kernel,
        out_shape=jax.ShapeDtypeStruct((32, 16, 512), jnp.bfloat16),
        in_specs=[VM], out_specs=VM,
        scratch_shapes=[dma((3,)), dma((3,)), dma],
        compiler_params=pltpu.CompilerParams(collective_id=3, has_side_effects=True, vmem_limit_bytes=LIMIT),
    )(cur)


def swap(x, cid):
    dma = pltpu.SemaphoreType.DMA
    return pl.pallas_call(
        swap_kernel,
        out_shape=jax.ShapeDtypeStruct(x.shape, x.dtype),
        in_specs=[VM], out_specs=VM,
        scratch_shapes=[dma, dma, dma],
        compiler_params=pltpu.CompilerParams(collective_id=cid, has_side_effects=True, vmem_limit_bytes=LIMIT),
    )(x)


def norm(values, gain, offset):
    center = jnp.mean(values, axis=0)
    spread = jnp.mean(values * values, axis=0) - center * center
    return (
        (values - center) * lax.rsqrt(spread + 1e-05) * gain[:, None, None] + offset[:, None, None]
    ).astype(jnp.bfloat16)


def per_device(
    pair, residue_mask, chain_ids, pair_gain, pair_bias, in_weight, gate_weight,
    hidden_gain, hidden_bias, cross_gain, out_weight,
):
    r = lax.axis_index("rows")
    c = lax.axis_index("ch")
    small = jnp.concatenate([hidden_gain, hidden_bias, cross_gain, jnp.zeros_like(cross_gain)], 0)
    small = jnp.pad(small, ((0, 0), (0, 96)))
    cur, win, wgate, small_all = gather(
        pair, jnp.swapaxes(in_weight, 2, 3).reshape(8, 32, 128), jnp.swapaxes(gate_weight, 1, 2), small
    )
    small_all = jnp.swapaxes(small_all[:, :, :32], 0, 1).reshape(8, 128)
    mask = residue_mask.astype(jnp.float32)
    rows = lambda a: lax.dynamic_slice_in_dim(a, r * 16, 16)
    cols = lambda a: lax.dynamic_slice_in_dim(a, c * 128, 128)
    pair_mask = rows(mask)[:, None] * cols(mask)[None, :]
    crossing = rows(chain_ids)[:, None] != cols(chain_ids)[None, :]
    for u in range(2):
        pair_f = cur.astype(jnp.float32)
        normed = norm(pair_f, pair_gain[u], pair_bias[u])
        proj = jnp.einsum("phc,cij->phij", win[4 * u : 4 * u + 4], normed, preferred_element_type=jnp.float32)
        factor = pair_mask[None] * jnp.where(crossing[None], small_all[4 + u][:, None, None], 1.0)
        left = (factor * jax.nn.sigmoid(proj[0]) * proj[1]).astype(jnp.bfloat16)
        right = (factor * jax.nn.sigmoid(proj[2]) * proj[3]).astype(jnp.bfloat16)
        both = swap(jnp.concatenate([left, right], 1), 1)
        both = both.reshape(32, 4, 2, 16, 128).transpose(2, 0, 3, 1, 4).reshape(2, 512, 512)
        tri = jnp.einsum(
            "ik,jk->ij" if u == 0 else "ki,kj->ij", both[0], both[1], preferred_element_type=jnp.float32
        ).astype(jnp.bfloat16)
        tri = swap(tri.reshape(32, 16, 4, 128).transpose(0, 2, 1, 3).reshape(128, 16, 128), 2)
        tri_normed = norm(tri.astype(jnp.float32), small_all[u], small_all[2 + u])
        gate = jax.nn.sigmoid(jnp.einsum("dc,cij->dij", wgate[u], normed, preferred_element_type=jnp.float32))
        update = jnp.einsum("hd,hij->dij", out_weight[u], tri_normed, preferred_element_type=jnp.float32)
        cur = (pair_f + gate * update).astype(jnp.bfloat16)
    return scatter(cur)


def solution(mesh):
    placed = (
        P("ch", "rows", None), P(), P(), P(), P(), P(None, None, None, "ch"), P(None, None, "ch"),
        P(None, "ch"), P(None, "ch"), P(None, "ch"), P(),
    )
    return jax.shard_map(
        per_device, mesh=mesh, in_specs=placed, out_specs=P("ch", "rows", None), check_vma=False
    )
```

time: 706 us -> 134 us (0.19)
  waiting for transfers between devices: 579 us -> 0 us
  Pallas kernels: 0 us -> 104 us
  matrix products: 62 us -> 3.58 us
  blocking collectives: 23.3 us -> 0 us
  between operations: 13.7 us -> 0.31 us
    all_gather x4 -> x0, waiting for transfers between devices: 343 us -> none  [the longest x2 285 us: apply_update(): lax.all_gather(right, 'rows', axis=1, tiled=True)]
    psum x4 -> x0, waiting for transfers between devices: 143 us -> none  [norm_local(): totals, squares = lax.psum((totals, squares), 'ch')]
    pallas_call x0 -> x6, Pallas kernels: none -> 104 us  [the longest x4 82.2 us: swap(): pl.pallas_call(swap_kernel, out_shape=jax.ShapeDtypeStruct(x.shape, x.dty...]
    reduce_scatter x2 -> x0, waiting for transfers between devices: 92.6 us -> none  [apply_update(): lax.psum_scatter(jnp.einsum('hd,hij->dij', weight_rows, tri_normed, prefe...]
    dot_general x8, matrix products: 62 us -> 3.58 us  [the longest x2 1.4 us: per_device(): jnp.einsum('phc,cij->phij', win[4 * u:4 * u + 4], normed, preferred_eleme...]
    all_to_all x1 -> x0, blocking collectives: 23.3 us -> none  [apply_update(): lax.all_to_all(left, 'rows', split_axis=2, concat_axis=1, tiled=True)]
  transfers between devices with their start and end apart: 10 -> 0, of which waited for: 10 -> 0; matrix products, arithmetic and copies ran while one was open for 2% -> 0% of each run, Pallas kernels for 0% -> 0%
where the time goes in v1:
time: 134 us; the launch traced here: 133 us
  Pallas kernels  104 us (78%)
  other arithmetic  13.4 us (10%)
  local copies, waits for them, and re-layouts  11.7 us (9%)
  matrix products  3.58 us (3%)
    pallas_call x4, Pallas kernels, swap(): pl.pallas_call(swap_kernel, out_shape=jax.ShapeDtypeStruct(x.shape, x.dty...  82.2 us
    pallas_call x1, Pallas kernels, gather(): pl.pallas_call(gather_kernel, out_shape=(shape((C, 16, 128), jnp.bfloat16...  13.6 us
    pallas_call x1, Pallas kernels, scatter(): pl.pallas_call(scatter_kernel, out_shape=jax.ShapeDtypeStruct((32, 16, 51...  8.56 us
    convert_element_type x2, other arithmetic, per_device(): left = (factor * jax.nn.sigmoid(proj[0]) * proj[1]).astype(jnp.bfloat16)  8.33 us
    unnamed x15, local copies, waits for them, and re-layouts  3.42 us
    slice x2, local copies, waits for them, and re-layouts, per_device(): left = (factor * jax.nn.sigmoid(proj[0]) * proj[1]).astype(jnp.bfloat16)  3.36 us

profile of v1, /device:TPU:1, one launch (start us, length us, event | category | flops | bytes accessed | tf_op | source)
XLA Modules:
  0.0 133.4 jit_solution(9798499138333855938)
XLA Ops:
  0.1 0.8 maximum_maximum_fusion
  0.9 1.0 copy-done
  1.9 0.8 copy-done.1
  2.8 0.7 copy-done.2
  3.5 13.6 %shard_map.109 = (bf16[128,16,128]{2,1,0:T(8,128)(2,1)S(1)}, bf16[8,128,128]{2,1,0:T(8,128)(2,1)S(1)}, bf16[2,128,128]{2,1,0:T(8,128)(2,1)S(1)}, f32[4,8,128]{2,1,0:T(8,128)S(1)}) custom-call(bf16[32,16,512]{2,1,0:T(8,128)(2,1)S(1)} %copy-done, bf16[8,32,128]{2,1,0:T(8,128)(2,1)S(1)} %bitcast.142, bf16[2,32,128]{2,1,0:T(8,128)(2,1)S(1)} %bitcast.143, ...), custom_call_target="tpu_custom_call" | custom-call | tf_op jit(solution)/shard_map/pallas_call | solution.py:111
  17.3 0.8 slice_bitcast_fusion.1
  18.4 0.7 fusion.66
  19.1 1.6 %fusion.92 = (f32[1,128,16,128]{3,1,2,0:T(8,128)S(1)}, f32[1,128,16,128]{3,1,2,0:T(8,128)S(1)}, f32[1,128,16,128]{3,1,2,0:T(8,128)}, f32[1,128,16,128]{3,1,2,0:T(8,128)}) fusion(f32[4,128,16,128]{3,1,2,0:T(8,128)S(1)} %fusion.66), kind=kLoop, calls=%fused_computation.147 | loop fusion | bytes 8388608 | tf_op jit(solution)/shard_map/slice | solution.py:175
  21.4 4.2 %fusion.44 = (bf16[128,16,128]{2,1,0:T(8,128)(2,1)S(1)}, bf16[128,16,128]{2,1,0:T(8,128)(2,1)S(1)}) fusion(f32[1,128,16,128]{3,1,2,0:T(8,128)} %get-tuple-element.34, f32[1,128,16,128]{3,1,2,0:T(8,128)S(1)} %get-tuple-element.32, f32[128]{0:T(128)S(1)} %broadcast_in_dim.52, f32[16,128]{1,0:T(8,128)S(1)} %broadcast_multiply_fusion, ...), kind=kLoop, calls=%fused_computation.69 | loop fusion | flops 3670016 | bytes 5253632 | tf_op jit(solution)/shard_map/convert_element_type | solution.py:175
  25.6 25.5 %shard_map.110 = bf16[128,32,128]{2,1,0:T(8,128)(2,1)S(1)} custom-call(bf16[128,32,128]{2,1,0:T(8,128)(2,1)S(1)} %pad_maximum_fusion.x), custom_call_target="tpu_custom_call" | custom-call | tf_op jit(solution)/shard_map/pallas_call | solution.py:136
  51.2 0.5 copy.199
  51.7 0.6 fusion.94
  53.0 16.4 %shard_map.111 = bf16[128,16,128]{2,1,0:T(8,128)(2,1)S(1)} custom-call(bf16[128,16,128]{2,1,0:T(8,128)(2,1)S(1)} %bitcast.140), custom_call_target="tpu_custom_call" | custom-call | tf_op jit(solution)/shard_map/pallas_call | solution.py:136
  70.7 1.3 convert_reduce_fusion
  72.4 0.7 fusion.64
  73.1 1.7 %fusion.91 = (f32[1,128,16,128]{3,1,2,0:T(8,128)S(1)}, f32[1,128,16,128]{3,1,2,0:T(8,128)S(1)}, f32[1,128,16,128]{3,1,2,0:T(8,128)}, f32[1,128,16,128]{3,1,2,0:T(8,128)}) fusion(f32[4,128,16,128]{3,1,2,0:T(8,128)S(1)} %fusion.64), kind=kLoop, calls=%fused_computation.146 | loop fusion | bytes 8388608 | tf_op jit(solution)/shard_map/slice | solution.py:175
  74.9 4.2 %fusion.30 = (bf16[128,16,128]{2,1,0:T(8,128)(2,1)S(1)}, bf16[128,16,128]{2,1,0:T(8,128)(2,1)S(1)}) fusion(f32[1,128,16,128]{3,1,2,0:T(8,128)} %get-tuple-element.30, f32[1,128,16,128]{3,1,2,0:T(8,128)S(1)} %get-tuple-element.28, f32[128]{0:T(128)S(1)} %broadcast_in_dim.54, f32[16,128]{1,0:T(8,128)S(1)} %broadcast_multiply_fusion, ...), kind=kLoop, calls=%fused_computation.51 | loop fusion | flops 3670016 | bytes 5253632 | tf_op jit(solution)/shard_map/convert_element_type | solution.py:175
  79.2 23.5 %shard_map.112 = bf16[128,32,128]{2,1,0:T(8,128)(2,1)S(1)} custom-call(bf16[128,32,128]{2,1,0:T(8,128)(2,1)S(1)} %pad_maximum_fusion.1.x), custom_call_target="tpu_custom_call" | custom-call | tf_op jit(solution)/shard_map/pallas_call | solution.py:136
  102.7 0.5 copy.198
  103.3 0.6 fusion.93
  104.6 16.8 %shard_map.113 = bf16[128,16,128]{2,1,0:T(8,128)(2,1)S(1)} custom-call(bf16[128,16,128]{2,1,0:T(8,128)(2,1)S(1)} %bitcast.141), custom_call_target="tpu_custom_call" | custom-call | tf_op jit(solution)/shard_map/pallas_call | solution.py:136
  123.3 0.8 fusion.21.cur
  124.1 8.6 %shard_map.114 = bf16[32,16,512]{2,1,0:T(8,128)(2,1)S(1)} custom-call(bf16[128,16,128]{2,1,0:T(8,128)(2,1)S(1)} %fusion.21.cur), custom_call_target="tpu_custom_call" | custom-call | tf_op jit(solution)/shard_map/pallas_call | solution.py:125
  132.6 0.8 copy.201
  (53 shorter events, 6.3 us)
Async XLA Ops:
  0.9 1.0 copy-start
  1.9 0.8 copy-start.1
  2.8 0.7 copy-start.2
  19.1 1.7 %copy-start.5 = (s32[512]{0:T(512)S(1)}, s32[512]{0:T(512)}, u32[]{:S(2)}) copy-start(s32[512]{0:T(512)} %param.12) | copy-start | bytes 6148
  19.1 1.9 %copy-start.6 = (s32[512]{0:T(512)S(1)}, s32[512]{0:T(512)}, u32[]{:S(2)}) copy-start(s32[512]{0:T(512)} %param.13) | copy-start | bytes 6148
  51.7 18.4 %copy-start.3 = (bf16[2,128,128]{2,1,0:T(8,128)(2,1)S(1)}, bf16[2,128,128]{2,1,0:T(8,128)(2,1)}, u32[]{:S(2)}) copy-start(bf16[2,128,128]{2,1,0:T(8,128)(2,1)} %param.21) | copy-start | bytes 196612
  103.3 18.8 %copy-start.4 = (bf16[2,128,128]{2,1,0:T(8,128)(2,1)S(1)}, bf16[2,128,128]{2,1,0:T(8,128)(2,1)}, u32[]{:S(2)}) copy-start(bf16[2,128,128]{2,1,0:T(8,128)(2,1)} %param.21) | copy-start | bytes 196612

commit v2 on v0

v2 whole, which is shorter than its diff:
```python
import jax
import jax.numpy as jnp
from jax import lax
from jax.experimental import pallas as pl
from jax.experimental.pallas import tpu as pltpu
from jax.sharding import PartitionSpec as P

MESH = pl.DeviceIdType.MESH
VM = pl.BlockSpec(memory_space=pltpu.VMEM)
ANY = pl.BlockSpec(memory_space=pl.ANY)
F32 = jnp.float32
BF16 = jnp.bfloat16


def aligned(index, size):
    return pl.ds(pl.multiple_of(index * size, size), size)


def sigmoid(v):
    return 0.5 * jnp.tanh(0.5 * v) + 0.5


def norm(v, gain, offset):
    center = jnp.mean(v, axis=0, keepdims=True)
    spread = jnp.mean(v * v, axis=0, keepdims=True) - center * center
    return (v - center) * lax.rsqrt(spread + 1e-05) * gain + offset


def columns(row):
    return jnp.broadcast_to(row, (128, 128)).T


def dot(a, b, dims=((1,), (0,))):
    return lax.dot_general(a, b, (dims, ((), ())), preferred_element_type=F32)


def kernel(
    pair, win, wgate, wout, pgain, pbias, hgain, hbias, cgain, mask, chain, out,
    pbuf, win_all, wgate_all, wout_t, mysmall, small_all, par, edge, turn, turn_lr,
    cur, normed, gate, stage, lr, tbuf, tri, obuf,
    p_send, p_recv, p_own, w_send, w_recv, w_own, lr_send, lr_recv, t_send, t_recv, o_send, o_recv, o_own, ready,
):
    r = lax.axis_index("rows")
    c = lax.axis_index("ch")
    x = lax.div(r, 8)
    zy = lax.rem(r, 8)
    y = lax.rem(zy, 4)
    spot = zy * 4 + c
    group = lax.rem(x + y, 4)
    mine = group * 32 + spot
    peers = [lax.rem(c + s, 4) for s in (1, 2, 3)]

    def place(turned, s):
        g = lax.rem(group + turned, 4)
        m = lax.rem(spot + s, 32)
        zy2 = lax.div(m, 4)
        x2 = lax.rem(g + 4 - lax.rem(zy2, 4), 4)
        return g * 32 + m, x2 * 8 + zy2, lax.rem(m, 4)

    barrier = pltpu.get_barrier_semaphore()
    for c2 in peers:
        pl.semaphore_signal(barrier, inc=1, device_id=(r, c2), device_id_type=MESH)

    @pl.loop(1, 32)
    def _(s):
        pl.semaphore_signal(barrier, inc=1, device_id=(lax.rem(r + s, 32), c), device_id_type=MESH)

    mysmall[...] = jnp.zeros_like(mysmall)
    mysmall[0:2, 0:32] = hgain[...]
    mysmall[2:4, 0:32] = hbias[...]
    mysmall[4:6, 0:32] = cgain[...]
    pl.semaphore_wait(barrier, 34)
    for c2 in peers:
        pl.semaphore_signal(ready, inc=1, device_id=(r, c2), device_id_type=MESH)

    def spread(k, src, dst, send, recv):
        copies = []
        for s, c2 in enumerate(peers):
            cp = pltpu.make_async_remote_copy(
                src_ref=src(c2), dst_ref=dst, send_sem=send.at[k, s], recv_sem=recv.at[k, s],
                device_id=(r, c2), device_id_type=MESH,
            )
            cp.start()
            copies.append(cp)
        return copies

    def own(k, src, dst, sem):
        cp = pltpu.make_async_copy(src, dst, sem.at[k])
        cp.start()
        return cp

    rows_c = aligned(c, 32)
    pair_c = lambda c2: pair.at[:, :, aligned(c2, 128)]
    moved = spread(0, pair_c, pbuf.at[rows_c], p_send, p_recv)
    moved_w0 = spread(0, lambda _: win.at[0], win_all.at[0, :, rows_c], w_send, w_recv)
    moved_sm = spread(1, lambda _: mysmall, small_all.at[c], w_send, w_recv)
    kept = own(0, pair_c(c), pbuf.at[rows_c], p_own)
    kept_w = [
        own(0, win.at[0], win_all.at[0, :, rows_c], w_own),
        own(1, mysmall, small_all.at[c], w_own),
        own(2, win.at[1], win_all.at[1, :, rows_c], w_own),
        own(3, wgate, wgate_all.at[:, rows_c], w_own),
    ]

    for u in range(2):
        par[u] = columns(pgain[u : u + 1, :])
        par[2 + u] = columns(pbias[u : u + 1, :])
        wout_t[u] = wout[u].astype(F32).T.astype(BF16)
    block = lax.div(r, 8)
    for k, ref in enumerate((mask, chain)):
        turn[128 * k : 128 * (k + 1), :] = columns(ref[pl.ds(block, 1), :].astype(F32))
    own_rows = lambda k: turn[pl.ds(pl.multiple_of(128 * k + lax.rem(r, 8) * 16, 16), 16), :]
    edge[0] = own_rows(0) * mask[pl.ds(c, 1), :].astype(F32)
    edge[1] = jnp.where(own_rows(1) != chain[pl.ds(c, 1), :].astype(F32), 1.0, 0.0)

    kept.wait()
    for cp in moved:
        cp.wait()
    turn[...] = pbuf[...].astype(F32).reshape(2048, 128)

    @pl.loop(0, 16)
    def _(i):
        v = turn[pl.ds(i, 128, stride=16), :]
        at = aligned(i, 128)
        cur[:, at] = v
        normed[:, at] = norm(v, par[0], par[2]).astype(BF16)

    for cp in kept_w[:2] + moved_sm:
        cp.wait()
    lanes = lax.broadcasted_iota(jnp.int32, (8, 128), 1)
    smalls = small_all[0]
    for c2 in (1, 2, 3):
        smalls = jnp.where(lanes >= 32 * c2, pltpu.roll(small_all[c2], 32 * c2, 1), smalls)
    for k in range(6):
        par[4 + k] = columns(smalls[k : k + 1, :])
    for cp in moved_w0:
        cp.wait()
    pl.semaphore_wait(ready, 3)

    later = []
    for u in range(2):
        @pl.loop(0, 4)
        def _(q, u=u):
            g = lax.rem(group + q, 4)
            rows_g = aligned(g, 32)
            weight = win_all[u, :, rows_g, :].reshape(128, 128)
            cross = par[8 + u, rows_g, :]

            @pl.loop(0, 8)
            def _(b):
                proj = dot(weight, normed[:, aligned(b, 256)])
                left = sigmoid(proj[0:32]) * proj[32:64]
                right = sigmoid(proj[64:96]) * proj[96:128]
                for k in range(2):
                    i = 2 * b + k
                    factor = edge[0, pl.ds(i, 1), :] * jnp.where(edge[1, pl.ds(i, 1), :] > 0.5, cross, 1.0)
                    half = slice(128 * k, 128 * (k + 1))
                    turn_lr[pl.ds(i, 32, stride=16), :] = factor * left[:, half]
                    turn_lr[pl.ds(512 + i, 32, stride=16), :] = factor * right[:, half]

            for k in range(2):
                stage[u, rows_g, k] = turn_lr[512 * k : 512 * (k + 1), :].astype(BF16).reshape(32, 16, 128)

            @pl.loop(jnp.where(q == 0, 1, 0), 32)
            def _(s):
                h2, r2, c2 = place(q, s)
                pltpu.make_async_remote_copy(
                    src_ref=stage.at[u, h2], dst_ref=lr.at[u, :, aligned(r, 16), aligned(c, 128)],
                    send_sem=lr_send.at[u], recv_sem=lr_recv.at[u], device_id=(r2, c2), device_id_type=MESH,
                ).start()

        pltpu.make_async_copy(
            stage.at[u, mine], lr.at[u, :, aligned(r, 16), aligned(c, 128)], lr_recv.at[u]
        ).start()
        if u == 0:
            moved_g = spread(2, lambda _: wgate, wgate_all.at[:, rows_c], w_send, w_recv)
            moved_w1 = spread(3, lambda _: win.at[1], win_all.at[1, :, rows_c], w_send, w_recv)
            for cp in kept_w[2:] + moved_g + moved_w1:
                cp.wait()

        @pl.loop(0, 8)
        def _(b, u=u):
            at = aligned(b, 256)
            gate[:, at] = sigmoid(dot(wgate_all[u], normed[:, at]))

        whole = pltpu.make_async_remote_copy(
            src_ref=stage.at[u, pl.ds(0, 127)], dst_ref=lr.at[u], send_sem=lr_send.at[u], recv_sem=lr_recv.at[u],
            device_id=(r, peers[0]), device_id_type=MESH,
        )
        whole.wait_recv()
        later.append(whole)

        @pl.loop(0, 4)
        def _(q, u=u):
            at = aligned(q, 128)
            if u == 0:
                part = dot(lr[u, 0, at, :], lr[u, 1], ((1,), (1,)))
            else:
                part = dot(lr[u, 0, :, at], lr[u, 1], ((0,), (0,)))
            tbuf[u, at, :] = part.astype(BF16)

        @pl.loop(0, 4)
        def _(q, u=u):
            @pl.loop(jnp.where(q == 0, 1, 0), 32)
            def _(s):
                _, r2, c2 = place(q, s)
                pltpu.make_async_remote_copy(
                    src_ref=tbuf.at[u, aligned(r2, 16), aligned(c2, 128)], dst_ref=tri.at[u, mine],
                    send_sem=t_send.at[u], recv_sem=t_recv.at[u], device_id=(r2, c2), device_id_type=MESH,
                ).start()

        pltpu.make_async_copy(
            tbuf.at[u, aligned(r, 16), aligned(c, 128)], tri.at[u, mine], t_recv.at[u]
        ).start()
        pltpu.make_async_remote_copy(
            src_ref=tri.at[u], dst_ref=tri.at[u], send_sem=t_send.at[u], recv_sem=t_recv.at[u],
            device_id=(r, peers[0]), device_id_type=MESH,
        ).wait_recv()
        later.append(
            pltpu.make_async_remote_copy(
                src_ref=tri.at[u, pl.ds(0, 127)], dst_ref=tri.at[u, pl.ds(0, 127)], send_sem=t_send.at[u],
                recv_sem=t_recv.at[u], device_id=(r, peers[0]), device_id_type=MESH,
            )
        )
        turn[...] = tri[u].astype(F32).reshape(2048, 128)

        @pl.loop(0, 8)
        def _(b, u=u):
            at = aligned(b, 256)
            halves = [
                norm(turn[pl.ds(2 * b + k, 128, stride=16), :], par[4 + u], par[6 + u]).astype(BF16) for k in range(2)
            ]
            update = dot(wout_t[u], jnp.concatenate(halves, axis=1))
            new = (cur[:, at] + gate[:, at] * update).astype(BF16).astype(F32)
            if u == 0:
                cur[:, at] = new
                for k in range(2):
                    at2 = aligned(2 * b + k, 128)
                    half = new[:, 128 * k : 128 * (k + 1)]
                    normed[:, at2] = norm(half, par[1], par[3]).astype(BF16)
            else:
                for k in range(2):
                    turn[pl.ds(2 * b + k, 128, stride=16), :] = new[:, 128 * k : 128 * (k + 1)]

    obuf[...] = turn[...].astype(BF16).reshape(128, 16, 128)
    here = out.at[:, :, aligned(c, 128)]
    last = spread(0, lambda c2: obuf.at[aligned(c2, 32)], here, o_send, o_recv)
    own(0, obuf.at[rows_c], here, o_own).wait()
    for cp in last:
        cp.wait()
    for cp in later:
        cp.wait_send()


def per_device(
    pair, residue_mask, chain_ids, pair_gain, pair_bias, in_weight, gate_weight,
    hidden_gain, hidden_bias, cross_gain, out_weight,
):
    dma = pltpu.SemaphoreType.DMA
    return pl.pallas_call(
        kernel,
        out_shape=jax.ShapeDtypeStruct((32, 16, 512), BF16),
        in_specs=[ANY, ANY, ANY] + [VM] * 8,
        out_specs=ANY,
        scratch_shapes=[
            pltpu.VMEM((128, 16, 128), BF16),
            pltpu.VMEM((2, 4, 128, 128), BF16),
            pltpu.VMEM((2, 128, 128), BF16),
            pltpu.VMEM((2, 128, 128), BF16),
            pltpu.VMEM((8, 128), F32),
            pltpu.VMEM((4, 8, 128), F32),
            pltpu.VMEM((10, 128, 128), F32),
            pltpu.VMEM((2, 16, 128), F32),
            pltpu.VMEM((2048, 128), F32),
            pltpu.VMEM((1024, 128), F32),
            pltpu.VMEM((128, 2048), F32),
            pltpu.VMEM((128, 2048), BF16),
            pltpu.VMEM((128, 2048), F32),
            pltpu.VMEM((2, 128, 2, 16, 128), BF16),
            pltpu.VMEM((2, 2, 512, 512), BF16),
            pltpu.VMEM((2, 512, 512), BF16),
            pltpu.VMEM((2, 128, 16, 128), BF16),
            pltpu.VMEM((128, 16, 128), BF16),
            dma((1, 3)), dma((1, 3)), dma((1,)),
            dma((4, 3)), dma((4, 3)), dma((4,)),
            dma((2,)), dma((2,)), dma((2,)), dma((2,)),
            dma((1, 3)), dma((1, 3)), dma((1,)),
            pltpu.SemaphoreType.REGULAR,
        ],
        compiler_params=pltpu.CompilerParams(
            collective_id=0, has_side_effects=True, vmem_limit_bytes=48 * 2**20
        ),
    )(
        pair,
        jnp.swapaxes(in_weight, 2, 3),
        jnp.swapaxes(gate_weight, 1, 2),
        out_weight,
        pair_gain, pair_bias, hidden_gain, hidden_bias, cross_gain,
        residue_mask.reshape(4, 128), chain_ids.reshape(4, 128),
    )


def solution(mesh):
    placed = (
        P("ch", "rows", None), P(), P(), P(), P(), P(None, None, None, "ch"), P(None, None, "ch"),
        P(None, "ch"), P(None, "ch"), P(None, "ch"), P(),
    )
    return jax.shard_map(
        per_device, mesh=mesh, in_specs=placed, out_specs=P("ch", "rows", None), check_vma=False
    )
```

time: 706 us -> 98.1 us (0.14)
  waiting for transfers between devices: 579 us -> 0 us
  Pallas kernels: 0 us -> 91.4 us
  matrix products: 62 us -> 0 us
  blocking collectives: 23.3 us -> 0 us
  between operations: 13.7 us -> 0.04 us
  other arithmetic: 13.5 us -> 0 us
  local copies, waits for them, and re-layouts: 14.3 us -> 6.31 us
    all_gather x4 -> x0, waiting for transfers between devices: 343 us -> none  [the longest x2 285 us: apply_update(): lax.all_gather(right, 'rows', axis=1, tiled=True)]
    psum x4 -> x0, waiting for transfers between devices: 143 us -> none  [norm_local(): totals, squares = lax.psum((totals, squares), 'ch')]
    reduce_scatter x2 -> x0, waiting for transfers between devices: 92.6 us -> none  [apply_update(): lax.psum_scatter(jnp.einsum('hd,hij->dij', weight_rows, tri_normed, prefe...]
    pallas_call x0 -> x1, Pallas kernels: none -> 91.4 us  [per_device(): pl.pallas_call(kernel, out_shape=jax.ShapeDtypeStruct((32, 16, 512), BF16...]
    dot_general x8 -> x0, matrix products: 62 us -> none  [the longest x1 30.2 us: apply_update(): jnp.einsum('hik,hjk->hij', left, lax.all_gather(right, 'rows', axis=1, ti...]
    all_to_all x1 -> x0, blocking collectives: 23.3 us -> none  [apply_update(): lax.all_to_all(left, 'rows', split_axis=2, concat_axis=1, tiled=True)]
    convert_element_type x7 -> x0, other arithmetic: 7.37 us -> none  [the longest x4 3.69 us: norm_local(): return ((values - center) * lax.rsqrt(spread + 1e-05) * gain[:, None, Non...]
  transfers between devices with their start and end apart: 10 -> 0, of which waited for: 10 -> 0; matrix products, arithmetic and copies ran while one was open for 2% -> 0% of each run, Pallas kernels for 0% -> 0%
where the time goes in v2:
time: 98.1 us; the launch traced here: 97.8 us
  Pallas kernels  91.4 us (93%)
  local copies, waits for them, and re-layouts  6.31 us (6%)
    pallas_call x1, Pallas kernels, per_device(): pl.pallas_call(kernel, out_shape=jax.ShapeDtypeStruct((32, 16, 512), BF16...  91.4 us
    unnamed x23, local copies, waits for them, and re-layouts  6.31 us

profile of v2, /device:TPU:1, one launch (start us, length us, event | category | flops | bytes accessed | tf_op | source)
XLA Modules:
  0.0 97.8 jit_solution(14425517143985546003)
XLA Ops:
  0.0 0.0 copy-start.7
  0.0 0.0 copy-start.8
  0.0 0.0 copy-start.5
  0.0 0.0 copy-start.4
  0.0 0.0 copy-start.6
  0.0 0.7 copy-done.7
  0.7 0.0 copy-done.8
  0.7 0.0 copy-done.5
  0.7 0.0 copy-done.4
  0.7 0.0 copy-done.6
  0.7 0.0 copy-start
  0.7 1.0 %copy-done = bf16[32,16,512]{2,1,0:T(8,128)(2,1)S(1)} copy-done((bf16[32,16,512]{2,1,0:T(8,128)(2,1)S(1)}, bf16[32,16,512]{2,1,0:T(8,128)(2,1)}, u32[]{:S(2)}) %copy-start) | copy-done | bytes 524312
  1.8 0.0 copy-start.1
  1.8 0.8 copy-done.1
  2.6 0.0 copy-start.2
  2.6 0.8 copy-done.2
  3.5 0.0 copy-start.3
  3.5 0.7 copy-done.3
  4.2 0.0 copy-start.9
  4.2 0.7 copy-done.9
  4.9 0.0 copy-start.10
  4.9 0.7 copy-done.10
  5.5 91.4 %shard_map.109 = bf16[32,16,512]{2,1,0:T(8,128)(2,1)S(1)} custom-call(bf16[32,16,512]{2,1,0:T(8,128)(2,1)S(1)} %copy-done, bf16[2,4,32,128]{3,2,1,0:T(8,128)(2,1)S(1)} %bitcast.4, bf16[2,32,128]{2,1,0:T(8,128)(2,1)S(1)} %bitcast.5, bf16[2,128,128]{2,1,0:T(8,128)(2,1)S(1)} %copy-done.2, f32[2,128]{1,0:T(2,128)S(1)} %copy-done.6, f32[2,128]{1,0:T(2,128)S(1)} %copy-done.7, ...), custom_call_target="tpu_custom_call" | custom-call | tf_op jit(solution)/shard_map/pallas_call | solution.py:260
  97.0 0.8 copy.13
Async XLA Ops:
  0.0 0.7 copy-start.7
  0.0 0.7 copy-start.8
  0.0 0.7 copy-start.5
  0.0 0.7 copy-start.4
  0.0 0.7 copy-start.6
  0.7 1.0 %copy-start = (bf16[32,16,512]{2,1,0:T(8,128)(2,1)S(1)}, bf16[32,16,512]{2,1,0:T(8,128)(2,1)}, u32[]{:S(2)}) copy-start(bf16[32,16,512]{2,1,0:T(8,128)(2,1)} %pair.1) | copy-start | bytes 1572868
  1.8 0.8 copy-start.1
  2.6 0.8 copy-start.2
  3.5 0.7 copy-start.3
  4.2 0.7 copy-start.9
  4.9 0.7 copy-start.10

commit v3 on v2

--- a/solution.py
+++ b/solution.py
@@ -6,7 +6,6 @@
 from jax.sharding import PartitionSpec as P
 
 MESH = pl.DeviceIdType.MESH
-VM = pl.BlockSpec(memory_space=pltpu.VMEM)
 ANY = pl.BlockSpec(memory_space=pl.ANY)
 F32 = jnp.float32
 BF16 = jnp.bfloat16
@@ -35,10 +34,11 @@
 
 
 def kernel(
-    pair, win, wgate, wout, pgain, pbias, hgain, hbias, cgain, mask, chain, out,
+    pair, win, wgate, wout_hbm, pgain_hbm, pbias_hbm, hgain_hbm, hbias_hbm, cgain_hbm, mask_hbm, chain_hbm, out,
+    wout, pgain, pbias, hgain, hbias, cgain, mask, chain,
     pbuf, win_all, wgate_all, wout_t, mysmall, small_all, par, edge, turn, turn_lr,
     cur, normed, gate, stage, lr, tbuf, tri, obuf,
-    p_send, p_recv, p_own, w_send, w_recv, w_own, lr_send, lr_recv, t_send, t_recv, o_send, o_recv, o_own, ready,
+    p_send, p_recv, p_own, w_send, w_recv, w_own, lr_send, lr_recv, t_send, t_recv, o_send, o_recv, o_own, f_own, ready,
 ):
     r = lax.axis_index("rows")
     c = lax.axis_index("ch")
@@ -57,6 +57,15 @@
         x2 = lax.rem(g + 4 - lax.rem(zy2, 4), 4)
         return g * 32 + m, x2 * 8 + zy2, lax.rem(m, 4)
 
+    fetched = [
+        pltpu.make_async_copy(a, b, f_own.at[k])
+        for k, (a, b) in enumerate((
+            (hgain_hbm, hgain), (hbias_hbm, hbias), (cgain_hbm, cgain), (pgain_hbm, pgain),
+            (pbias_hbm, pbias), (mask_hbm, mask), (chain_hbm, chain), (wout_hbm, wout),
+        ))
+    ]
+    for cp in fetched:
+        cp.start()
     barrier = pltpu.get_barrier_semaphore()
     for c2 in peers:
         pl.semaphore_signal(barrier, inc=1, device_id=(r, c2), device_id_type=MESH)
@@ -65,6 +74,8 @@
     def _(s):
         pl.semaphore_signal(barrier, inc=1, device_id=(lax.rem(r + s, 32), c), device_id_type=MESH)
 
+    for cp in fetched[:3]:
+        cp.wait()
     mysmall[...] = jnp.zeros_like(mysmall)
     mysmall[0:2, 0:32] = hgain[...]
     mysmall[2:4, 0:32] = hbias[...]
@@ -102,6 +113,8 @@
         own(3, wgate, wgate_all.at[:, rows_c], w_own),
     ]
 
+    for cp in fetched[3:]:
+        cp.wait()
     for u in range(2):
         par[u] = columns(pgain[u : u + 1, :])
         par[2 + u] = columns(pbias[u : u + 1, :])
@@ -260,9 +273,17 @@
     return pl.pallas_call(
         kernel,
         out_shape=jax.ShapeDtypeStruct((32, 16, 512), BF16),
-        in_specs=[ANY, ANY, ANY] + [VM] * 8,
+        in_specs=[ANY] * 11,
         out_specs=ANY,
         scratch_shapes=[
+            pltpu.VMEM((2, 128, 128), BF16),
+            pltpu.VMEM((2, 128), F32),
+            pltpu.VMEM((2, 128), F32),
+            pltpu.VMEM((2, 32), F32),
+            pltpu.VMEM((2, 32), F32),
+            pltpu.VMEM((2, 32), F32),
+            pltpu.VMEM((4, 128), jnp.int32),
+            pltpu.VMEM((4, 128), jnp.int32),
             pltpu.VMEM((128, 16, 128), BF16),
             pltpu.VMEM((2, 4, 128, 128), BF16),
             pltpu.VMEM((2, 128, 128), BF16),
@@ -284,11 +305,11 @@
             dma((1, 3)), dma((1, 3)), dma((1,)),
             dma((4, 3)), dma((4, 3)), dma((4,)),
             dma((2,)), dma((2,)), dma((2,)), dma((2,)),
-            dma((1, 3)), dma((1, 3)), dma((1,)),
+            dma((1, 3)), dma((1, 3)), dma((1,)), dma((8,)),
             pltpu.SemaphoreType.REGULAR,
         ],
         compiler_params=pltpu.CompilerParams(
-            collective_id=0, has_side_effects=True, vmem_limit_bytes=48 * 2**20
+            collective_id=0, has_side_effects=True, vmem_limit_bytes=62 * 2**20
         ),
     )(
         pair,

time: 98.1 us -> 94.1 us (0.959)
  local copies, waits for them, and re-layouts: 6.31 us -> 1.87 us
    unnamed x23 -> x1, local copies, waits for them, and re-layouts: 6.31 us -> 1.87 us
where the time goes in v3:
time: 94.1 us; the launch traced here: 93.9 us
  Pallas kernels  92 us (98%)
  local copies, waits for them, and re-layouts  1.87 us (2%)
    pallas_call x1, Pallas kernels, per_device(): pl.pallas_call(kernel, out_shape=jax.ShapeDtypeStruct((32, 16, 512), BF16...  92 us

profile of v3, /device:TPU:1, one launch (start us, length us, event | category | flops | bytes accessed | tf_op | source)
XLA Modules:
  0.0 93.9 jit_solution(1894823451297660324)
XLA Ops:
  0.0 92.0 %shard_map.109 = bf16[32,16,512]{2,1,0:T(8,128)(2,1)} custom-call(bf16[32,16,512]{2,1,0:T(8,128)(2,1)} %pair.1, bf16[2,4,32,128]{3,2,1,0:T(8,128)(2,1)} %bitcast.4, bf16[2,32,128]{2,1,0:T(8,128)(2,1)} %bitcast.5, bf16[2,128,128]{2,1,0:T(8,128)(2,1)} %wout_hbm.1, f32[2,128]{1,0:T(2,128)} %pgain_hbm.1, f32[2,128]{1,0:T(2,128)} %pbias_hbm.1, ...), custom_call_target="tpu_custom_call" | custom-call | tf_op jit(solution)/shard_map/pallas_call | solution.py:273
  92.0 1.9 %copy.13 = bf16[32,16,512]{2,1,0:T(8,128)(2,1)} copy(bf16[32,16,512]{2,1,0:T(8,128)(2,1)} %shard_map.109) | data formatting | bytes 1048576

commit v4 on v3

--- a/solution.py
+++ b/solution.py
@@ -50,12 +50,21 @@
     mine = group * 32 + spot
     peers = [lax.rem(c + s, 4) for s in (1, 2, 3)]
 
-    def place(turned, s):
-        g = lax.rem(group + turned, 4)
-        m = lax.rem(spot + s, 32)
-        zy2 = lax.div(m, 4)
-        x2 = lax.rem(g + 4 - lax.rem(zy2, 4), 4)
-        return g * 32 + m, x2 * 8 + zy2, lax.rem(m, 4)
+    turned = [lax.rem(c + k, 4) for k in range(4)]
+
+    def each(q, send):
+        g = lax.rem(group + q, 4)
+
+        def line(j, skip):
+            zy2 = lax.rem(zy + j, 8)
+            r2 = lax.rem(g + 4 - lax.rem(zy2, 4), 4) * 8 + zy2
+            for k in range(skip, 4):
+                send(g * 32 + zy2 * 4 + turned[k], r2, turned[k])
+
+        line(0, 1 if q == 0 else 0)
+        @pl.loop(1, 8)
+        def _(j):
+            line(j, 0)
 
     fetched = [
         pltpu.make_async_copy(a, b, f_own.at[k])
@@ -70,9 +79,11 @@
     for c2 in peers:
         pl.semaphore_signal(barrier, inc=1, device_id=(r, c2), device_id_type=MESH)
 
-    @pl.loop(1, 32)
-    def _(s):
-        pl.semaphore_signal(barrier, inc=1, device_id=(lax.rem(r + s, 32), c), device_id_type=MESH)
+    x_peers = [lax.rem(x + k, 4) * 8 + zy for k in (1, 2, 3)]
+    y_peers = [r - y + lax.rem(y + k, 4) for k in (1, 2, 3)]
+    z_peers = [x * 8 + lax.rem(zy + 4, 8)]
+    for r2 in x_peers + y_peers + z_peers:
+        pl.semaphore_signal(barrier, inc=1, device_id=(r2, c), device_id_type=MESH)
 
     for cp in fetched[:3]:
         cp.wait()
@@ -80,9 +91,7 @@
     mysmall[0:2, 0:32] = hgain[...]
     mysmall[2:4, 0:32] = hbias[...]
     mysmall[4:6, 0:32] = cgain[...]
-    pl.semaphore_wait(barrier, 34)
-    for c2 in peers:
-        pl.semaphore_signal(ready, inc=1, device_id=(r, c2), device_id_type=MESH)
+    pl.semaphore_wait(barrier, 10)
 
     def spread(k, src, dst, send, recv):
         copies = []
@@ -105,6 +114,8 @@
     moved = spread(0, pair_c, pbuf.at[rows_c], p_send, p_recv)
     moved_w0 = spread(0, lambda _: win.at[0], win_all.at[0, :, rows_c], w_send, w_recv)
     moved_sm = spread(1, lambda _: mysmall, small_all.at[c], w_send, w_recv)
+    moved_g = spread(2, lambda _: wgate, wgate_all.at[:, rows_c], w_send, w_recv)
+    moved_w1 = spread(3, lambda _: win.at[1], win_all.at[1, :, rows_c], w_send, w_recv)
     kept = own(0, pair_c(c), pbuf.at[rows_c], p_own)
     kept_w = [
         own(0, win.at[0], win_all.at[0, :, rows_c], w_own),
@@ -112,6 +123,11 @@
         own(2, win.at[1], win_all.at[1, :, rows_c], w_own),
         own(3, wgate, wgate_all.at[:, rows_c], w_own),
     ]
+
+    for k, known in enumerate((x_peers, y_peers, z_peers)):
+        for r2 in known:
+            pl.semaphore_signal(ready.at[k], inc=1, device_id=(r2, c), device_id_type=MESH)
+        pl.semaphore_wait(ready.at[k], len(known))
 
     for cp in fetched[3:]:
         cp.wait()
@@ -131,7 +147,7 @@
         cp.wait()
     turn[...] = pbuf[...].astype(F32).reshape(2048, 128)
 
-    @pl.loop(0, 16)
+    @pl.loop(0, 16, unroll=4)
     def _(i):
         v = turn[pl.ds(i, 128, stride=16), :]
         at = aligned(i, 128)
@@ -148,19 +164,17 @@
         par[4 + k] = columns(smalls[k : k + 1, :])
     for cp in moved_w0:
         cp.wait()
-    pl.semaphore_wait(ready, 3)
 
     later = []
     for u in range(2):
-        @pl.loop(0, 4)
-        def _(q, u=u):
+        for q in range(4):
             g = lax.rem(group + q, 4)
             rows_g = aligned(g, 32)
             weight = win_all[u, :, rows_g, :].reshape(128, 128)
             cross = par[8 + u, rows_g, :]
 
-            @pl.loop(0, 8)
-            def _(b):
+            @pl.loop(0, 8, unroll=8)
+            def _(b, u=u, weight=weight, cross=cross):
                 proj = dot(weight, normed[:, aligned(b, 256)])
                 left = sigmoid(proj[0:32]) * proj[32:64]
                 right = sigmoid(proj[64:96]) * proj[96:128]
@@ -174,24 +188,22 @@
             for k in range(2):
                 stage[u, rows_g, k] = turn_lr[512 * k : 512 * (k + 1), :].astype(BF16).reshape(32, 16, 128)
 
-            @pl.loop(jnp.where(q == 0, 1, 0), 32)
-            def _(s):
-                h2, r2, c2 = place(q, s)
+            def send_lr(h2, r2, c2, u=u):
                 pltpu.make_async_remote_copy(
                     src_ref=stage.at[u, h2], dst_ref=lr.at[u, :, aligned(r, 16), aligned(c, 128)],
                     send_sem=lr_send.at[u], recv_sem=lr_recv.at[u], device_id=(r2, c2), device_id_type=MESH,
                 ).start()
 
+            each(q, send_lr)
+
         pltpu.make_async_copy(
             stage.at[u, mine], lr.at[u, :, aligned(r, 16), aligned(c, 128)], lr_recv.at[u]
         ).start()
         if u == 0:
-            moved_g = spread(2, lambda _: wgate, wgate_all.at[:, rows_c], w_send, w_recv)
-            moved_w1 = spread(3, lambda _: win.at[1], win_all.at[1, :, rows_c], w_send, w_recv)
             for cp in kept_w[2:] + moved_g + moved_w1:
                 cp.wait()
 
-        @pl.loop(0, 8)
+        @pl.loop(0, 8, unroll=8)
         def _(b, u=u):
             at = aligned(b, 256)
             gate[:, at] = sigmoid(dot(wgate_all[u], normed[:, at]))
@@ -203,24 +215,17 @@
         whole.wait_recv()
         later.append(whole)
 
-        @pl.loop(0, 4)
-        def _(q, u=u):
-            at = aligned(q, 128)
-            if u == 0:
-                part = dot(lr[u, 0, at, :], lr[u, 1], ((1,), (1,)))
-            else:
-                part = dot(lr[u, 0, :, at], lr[u, 1], ((0,), (0,)))
-            tbuf[u, at, :] = part.astype(BF16)
-
-        @pl.loop(0, 4)
-        def _(q, u=u):
-            @pl.loop(jnp.where(q == 0, 1, 0), 32)
-            def _(s):
-                _, r2, c2 = place(q, s)
-                pltpu.make_async_remote_copy(
-                    src_ref=tbuf.at[u, aligned(r2, 16), aligned(c2, 128)], dst_ref=tri.at[u, mine],
-                    send_sem=t_send.at[u], recv_sem=t_recv.at[u], device_id=(r2, c2), device_id_type=MESH,
-                ).start()
+        dims = ((1,), (1,)) if u == 0 else ((0,), (0,))
+        tbuf[u] = dot(lr[u, 0], lr[u, 1], dims).astype(BF16)
+
+        def send_t(_, r2, c2, u=u):
+            pltpu.make_async_remote_copy(
+                src_ref=tbuf.at[u, aligned(r2, 16), aligned(c2, 128)], dst_ref=tri.at[u, mine],
+                send_sem=t_send.at[u], recv_sem=t_recv.at[u], device_id=(r2, c2), device_id_type=MESH,
+            ).start()
+
+        for q in range(4):
+            each(q, send_t)
 
         pltpu.make_async_copy(
             tbuf.at[u, aligned(r, 16), aligned(c, 128)], tri.at[u, mine], t_recv.at[u]
@@ -237,7 +242,7 @@
         )
         turn[...] = tri[u].astype(F32).reshape(2048, 128)
 
-        @pl.loop(0, 8)
+        @pl.loop(0, 8, unroll=8)
         def _(b, u=u):
             at = aligned(b, 256)
             halves = [
@@ -306,7 +311,7 @@
             dma((4, 3)), dma((4, 3)), dma((4,)),
             dma((2,)), dma((2,)), dma((2,)), dma((2,)),
             dma((1, 3)), dma((1, 3)), dma((1,)), dma((8,)),
-            pltpu.SemaphoreType.REGULAR,
+            pltpu.SemaphoreType.REGULAR((3,)),
         ],
         compiler_params=pltpu.CompilerParams(
             collective_id=0, has_side_effects=True, vmem_limit_bytes=62 * 2**20

time: 94.1 us -> 83.9 us (0.89)
  Pallas kernels: 92 us -> 81.9 us
    pallas_call x1, Pallas kernels: 92 us -> 81.9 us  [per_device(): pl.pallas_call(kernel, out_shape=jax.ShapeDtypeStruct((32, 16, 512), BF16...]
where the time goes in v4:
time: 83.9 us; the launch traced here: 83.7 us
  Pallas kernels  81.9 us (98%)
  local copies, waits for them, and re-layouts  1.87 us (2%)
    pallas_call x1, Pallas kernels, per_device(): pl.pallas_call(kernel, out_shape=jax.ShapeDtypeStruct((32, 16, 512), BF16...  81.9 us
    unnamed x1, local copies, waits for them, and re-layouts  1.87 us

profile of v4, /device:TPU:1, one launch (start us, length us, event | category | flops | bytes accessed | tf_op | source)
XLA Modules:
  0.0 83.7 jit_solution(17077944518594146821)
XLA Ops:
  0.0 81.9 %shard_map.109 = bf16[32,16,512]{2,1,0:T(8,128)(2,1)} custom-call(bf16[32,16,512]{2,1,0:T(8,128)(2,1)} %pair.1, bf16[2,4,32,128]{3,2,1,0:T(8,128)(2,1)} %bitcast.4, bf16[2,32,128]{2,1,0:T(8,128)(2,1)} %bitcast.5, bf16[2,128,128]{2,1,0:T(8,128)(2,1)} %wout_hbm.1, f32[2,128]{1,0:T(2,128)} %pgain_hbm.1, f32[2,128]{1,0:T(2,128)} %pbias_hbm.1, ...), custom_call_target="tpu_custom_call" | custom-call | tf_op jit(solution)/shard_map/pallas_call | solution.py:278
  81.9 1.9 %copy.13 = bf16[32,16,512]{2,1,0:T(8,128)(2,1)} copy(bf16[32,16,512]{2,1,0:T(8,128)(2,1)} %shard_map.109) | data formatting | bytes 1048576

commit v5 on v4

--- a/solution.py
+++ b/solution.py
@@ -1,3 +1,5 @@
+import functools
+
 import jax
 import jax.numpy as jnp
 from jax import lax
@@ -38,7 +40,7 @@
     wout, pgain, pbias, hgain, hbias, cgain, mask, chain,
     pbuf, win_all, wgate_all, wout_t, mysmall, small_all, par, edge, turn, turn_lr,
     cur, normed, gate, stage, lr, tbuf, tri, obuf,
-    p_send, p_recv, p_own, w_send, w_recv, w_own, lr_send, lr_recv, t_send, t_recv, o_send, o_recv, o_own, f_own, ready,
+    p_send, p_recv, p_own, w_send, w_recv, w_own, lr_send, first_recv, second_recv, t_send, t_recv, o_send, o_recv, o_own, f_own, ready,
 ):
     r = lax.axis_index("rows")
     c = lax.axis_index("ch")
@@ -48,23 +50,27 @@
     spot = zy * 4 + c
     group = lax.rem(x + y, 4)
     mine = group * 32 + spot
+    spot_row = group * 8 + zy
     peers = [lax.rem(c + s, 4) for s in (1, 2, 3)]
 
     turned = [lax.rem(c + k, 4) for k in range(4)]
 
-    def each(q, send):
-        g = lax.rem(group + q, 4)
-
+    def each(g, send, skip=0):
         def line(j, skip):
             zy2 = lax.rem(zy + j, 8)
             r2 = lax.rem(g + 4 - lax.rem(zy2, 4), 4) * 8 + zy2
             for k in range(skip, 4):
                 send(g * 32 + zy2 * 4 + turned[k], r2, turned[k])
 
-        line(0, 1 if q == 0 else 0)
+        line(0, skip)
+
         @pl.loop(1, 8)
         def _(j):
             line(j, 0)
+
+    def hidden_row(r2):
+        zy2 = lax.rem(r2, 8)
+        return lax.rem(lax.div(r2, 8) + zy2, 4) * 8 + zy2
 
     fetched = [
         pltpu.make_async_copy(a, b, f_own.at[k])
@@ -166,7 +172,24 @@
         cp.wait()
 
     later = []
+
+    def landing(u, k):
+        row = spot_row if (u, k) == (0, 0) else r
+        return lr.at[u, k, aligned(row, 16), aligned(c, 128)]
+
+    def send_lr(u, k, sem, h2, r2, c2):
+        pltpu.make_async_remote_copy(
+            src_ref=stage.at[u, h2, k], dst_ref=landing(u, k), send_sem=lr_send.at[u], recv_sem=sem,
+            device_id=(r2, c2), device_id_type=MESH,
+        ).start()
+
+    def arrived(src, dst, send, recv):
+        return pltpu.make_async_remote_copy(
+            src_ref=src, dst_ref=dst, send_sem=send, recv_sem=recv, device_id=(r, peers[0]), device_id_type=MESH
+        )
+
     for u in range(2):
+        first, second = (1, 0) if u == 0 else (0, 1)
         for q in range(4):
             g = lax.rem(group + q, 4)
             rows_g = aligned(g, 32)
@@ -188,17 +211,20 @@
             for k in range(2):
                 stage[u, rows_g, k] = turn_lr[512 * k : 512 * (k + 1), :].astype(BF16).reshape(32, 16, 128)
 
-            def send_lr(h2, r2, c2, u=u):
-                pltpu.make_async_remote_copy(
-                    src_ref=stage.at[u, h2], dst_ref=lr.at[u, :, aligned(r, 16), aligned(c, 128)],
-                    send_sem=lr_send.at[u], recv_sem=lr_recv.at[u], device_id=(r2, c2), device_id_type=MESH,
-                ).start()
-
-            each(q, send_lr)
-
-        pltpu.make_async_copy(
-            stage.at[u, mine], lr.at[u, :, aligned(r, 16), aligned(c, 128)], lr_recv.at[u]
-        ).start()
+            each(g, functools.partial(send_lr, u, first, first_recv.at[u]), 1 if q == 0 else 0)
+
+        for q in range(4):
+            if u == 0:
+                g = lax.rem(group + q, 4)
+                each(g, functools.partial(send_lr, u, second, second_recv.at[u, q]), 1 if q == 0 else 0)
+            else:
+                @pl.loop(1 if q == 0 else 0, 32)
+                def _(j, u=u, q=q):
+                    r2 = lax.rem(r + j, 32)
+                    send_lr(u, second, second_recv.at[u, q], hidden_row(r2) * 4 + turned[q], r2, turned[q])
+
+        for k, sem in ((first, first_recv.at[u]), (second, second_recv.at[u, 0])):
+            pltpu.make_async_copy(stage.at[u, mine, k], landing(u, k), sem).start()
         if u == 0:
             for cp in kept_w[2:] + moved_g + moved_w1:
                 cp.wait()
@@ -208,27 +234,35 @@
             at = aligned(b, 256)
             gate[:, at] = sigmoid(dot(wgate_all[u], normed[:, at]))
 
-        whole = pltpu.make_async_remote_copy(
-            src_ref=stage.at[u, pl.ds(0, 127)], dst_ref=lr.at[u], send_sem=lr_send.at[u], recv_sem=lr_recv.at[u],
-            device_id=(r, peers[0]), device_id_type=MESH,
-        )
-        whole.wait_recv()
-        later.append(whole)
-
-        dims = ((1,), (1,)) if u == 0 else ((0,), (0,))
-        tbuf[u] = dot(lr[u, 0], lr[u, 1], dims).astype(BF16)
+        arrived(lr.at[u, first], lr.at[u, first], lr_send.at[u], first_recv.at[u]).wait_recv()
+        later.append(arrived(stage.at[u, pl.ds(0, 127)], stage.at[u, pl.ds(0, 127)], lr_send.at[u], first_recv.at[u]))
 
         def send_t(_, r2, c2, u=u):
+            row = hidden_row(r2) if u == 0 else r2
             pltpu.make_async_remote_copy(
-                src_ref=tbuf.at[u, aligned(r2, 16), aligned(c2, 128)], dst_ref=tri.at[u, mine],
+                src_ref=tbuf.at[u, aligned(row, 16), aligned(c2, 128)], dst_ref=tri.at[u, mine],
                 send_sem=t_send.at[u], recv_sem=t_recv.at[u], device_id=(r2, c2), device_id_type=MESH,
             ).start()
 
         for q in range(4):
-            each(q, send_t)
+            if u == 0:
+                g = lax.rem(group + 4 - q, 4)
+                part = lr.at[0, 0, aligned(g, 128)]
+                arrived(part, part, lr_send.at[u], second_recv.at[u, q]).wait_recv()
+                tbuf[0, aligned(g, 128), :] = dot(part[...], lr[0, 1], ((1,), (1,))).astype(BF16)
+                each(g, send_t, 1 if q == 0 else 0)
+            else:
+                c2 = lax.rem(c + 4 - q, 4)
+                part = lr.at[1, 1, :, aligned(c2, 128)]
+                arrived(part, part, lr_send.at[u], second_recv.at[u, q]).wait_recv()
+                tbuf[1, :, aligned(c2, 128)] = dot(lr[1, 0], part[...], ((0,), (0,))).astype(BF16)
+
+                @pl.loop(1 if q == 0 else 0, 32)
+                def _(j, c2=c2, send_t=send_t):
+                    send_t(None, lax.rem(r + j, 32), c2)
 
         pltpu.make_async_copy(
-            tbuf.at[u, aligned(r, 16), aligned(c, 128)], tri.at[u, mine], t_recv.at[u]
+            tbuf.at[u, aligned(spot_row if u == 0 else r, 16), aligned(c, 128)], tri.at[u, mine], t_recv.at[u]
         ).start()
         pltpu.make_async_remote_copy(
             src_ref=tri.at[u], dst_ref=tri.at[u], send_sem=t_send.at[u], recv_sem=t_recv.at[u],
@@ -309,7 +343,7 @@
             pltpu.VMEM((128, 16, 128), BF16),
             dma((1, 3)), dma((1, 3)), dma((1,)),
             dma((4, 3)), dma((4, 3)), dma((4,)),
-            dma((2,)), dma((2,)), dma((2,)), dma((2,)),
+            dma((2,)), dma((2,)), dma((2, 4)), dma((2,)), dma((2,)),
             dma((1, 3)), dma((1, 3)), dma((1,)), dma((8,)),
             pltpu.SemaphoreType.REGULAR((3,)),
         ],

time: 83.9 us -> 77.9 us (0.928)
  Pallas kernels: 81.9 us -> 75.9 us
    pallas_call x1, Pallas kernels: 81.9 us -> 75.9 us  [per_device(): pl.pallas_call(kernel, out_shape=jax.ShapeDtypeStruct((32, 16, 512), BF16...]
where the time goes in v5:
time: 77.9 us; the launch traced here: 77.7 us
  Pallas kernels  75.9 us (97%)
  local copies, waits for them, and re-layouts  1.87 us (2%)
    pallas_call x1, Pallas kernels, per_device(): pl.pallas_call(kernel, out_shape=jax.ShapeDtypeStruct((32, 16, 512), BF16...  75.9 us
    unnamed x1, local copies, waits for them, and re-layouts  1.87 us

profile of v5, /device:TPU:1, one launch (start us, length us, event | category | flops | bytes accessed | tf_op | source)
XLA Modules:
  0.0 77.7 jit_solution(2714075462162317481)
XLA Ops:
  0.0 75.9 %shard_map.109 = bf16[32,16,512]{2,1,0:T(8,128)(2,1)} custom-call(bf16[32,16,512]{2,1,0:T(8,128)(2,1)} %pair.1, bf16[2,4,32,128]{3,2,1,0:T(8,128)(2,1)} %bitcast.4, bf16[2,32,128]{2,1,0:T(8,128)(2,1)} %bitcast.5, bf16[2,128,128]{2,1,0:T(8,128)(2,1)} %wout_hbm.1, f32[2,128]{1,0:T(2,128)} %pgain_hbm.1, f32[2,128]{1,0:T(2,128)} %pbias_hbm.1, ...), custom_call_target="tpu_custom_call" | custom-call | tf_op jit(solution)/shard_map/pallas_call | solution.py:312
  75.9 1.9 %copy.13 = bf16[32,16,512]{2,1,0:T(8,128)(2,1)} copy(bf16[32,16,512]{2,1,0:T(8,128)(2,1)} %shard_map.109) | data formatting | bytes 1048576

commit v6 on v5

--- a/solution.py
+++ b/solution.py
@@ -90,6 +90,14 @@
     z_peers = [x * 8 + lax.rem(zy + 4, 8)]
     for r2 in x_peers + y_peers + z_peers:
         pl.semaphore_signal(barrier, inc=1, device_id=(r2, c), device_id_type=MESH)
+    core = lax.rem(c, 2)
+    other = 2 - 2 * lax.div(c, 2)
+    facing = [other + core, other + 1 - core]
+    sibling = (r, 3 - other - core)
+    across = [(z_peers[0], c2) for c2 in facing]
+    w_peers = across + [sibling]
+    for dev in across:
+        pl.semaphore_signal(barrier, inc=1, device_id=dev, device_id_type=MESH)
 
     for cp in fetched[:3]:
         cp.wait()
@@ -97,14 +105,14 @@
     mysmall[0:2, 0:32] = hgain[...]
     mysmall[2:4, 0:32] = hbias[...]
     mysmall[4:6, 0:32] = cgain[...]
-    pl.semaphore_wait(barrier, 10)
-
-    def spread(k, src, dst, send, recv):
+    pl.semaphore_wait(barrier, 12)
+
+    def spread(k, src, dst, send, recv, devices):
         copies = []
-        for s, c2 in enumerate(peers):
+        for s, dev in enumerate(devices):
             cp = pltpu.make_async_remote_copy(
-                src_ref=src(c2), dst_ref=dst, send_sem=send.at[k, s], recv_sem=recv.at[k, s],
-                device_id=(r, c2), device_id_type=MESH,
+                src_ref=src(dev[1]), dst_ref=dst, send_sem=send.at[k, s], recv_sem=recv.at[k, s],
+                device_id=dev, device_id_type=MESH,
             )
             cp.start()
             copies.append(cp)
@@ -116,12 +124,13 @@
         return cp
 
     rows_c = aligned(c, 32)
+    c_peers = [(r, c2) for c2 in facing] + [sibling]
     pair_c = lambda c2: pair.at[:, :, aligned(c2, 128)]
-    moved = spread(0, pair_c, pbuf.at[rows_c], p_send, p_recv)
-    moved_w0 = spread(0, lambda _: win.at[0], win_all.at[0, :, rows_c], w_send, w_recv)
-    moved_sm = spread(1, lambda _: mysmall, small_all.at[c], w_send, w_recv)
-    moved_g = spread(2, lambda _: wgate, wgate_all.at[:, rows_c], w_send, w_recv)
-    moved_w1 = spread(3, lambda _: win.at[1], win_all.at[1, :, rows_c], w_send, w_recv)
+    moved = spread(0, pair_c, pbuf.at[rows_c], p_send, p_recv, c_peers)
+    moved_w0 = spread(0, lambda _: win.at[0], win_all.at[0, :, rows_c], w_send, w_recv, w_peers)
+    moved_sm = spread(1, lambda _: mysmall, small_all.at[c], w_send, w_recv, w_peers)
+    moved_g = spread(2, lambda _: wgate, wgate_all.at[:, rows_c], w_send, w_recv, w_peers)
+    moved_w1 = spread(3, lambda _: win.at[1], win_all.at[1, :, rows_c], w_send, w_recv, w_peers)
     kept = own(0, pair_c(c), pbuf.at[rows_c], p_own)
     kept_w = [
         own(0, win.at[0], win_all.at[0, :, rows_c], w_own),
@@ -296,7 +305,7 @@
 
     obuf[...] = turn[...].astype(BF16).reshape(128, 16, 128)
     here = out.at[:, :, aligned(c, 128)]
-    last = spread(0, lambda c2: obuf.at[aligned(c2, 32)], here, o_send, o_recv)
+    last = spread(0, lambda c2: obuf.at[aligned(c2, 32)], here, o_send, o_recv, c_peers)
     own(0, obuf.at[rows_c], here, o_own).wait()
     for cp in last:
         cp.wait()

time: 77.9 us -> 76.3 us (0.979)
  Pallas kernels: 75.9 us -> 74.2 us
    pallas_call x1, Pallas kernels: 75.9 us -> 74.2 us  [per_device(): pl.pallas_call(kernel, out_shape=jax.ShapeDtypeStruct((32, 16, 512), BF16...]
where the time goes in v6:
time: 76.3 us; the launch traced here: 76.1 us
  Pallas kernels  74.2 us (97%)
  local copies, waits for them, and re-layouts  1.87 us (2%)
    pallas_call x1, Pallas kernels, per_device(): pl.pallas_call(kernel, out_shape=jax.ShapeDtypeStruct((32, 16, 512), BF16...  74.2 us
    unnamed x1, local copies, waits for them, and re-layouts  1.87 us

profile of v6, /device:TPU:1, one launch (start us, length us, event | category | flops | bytes accessed | tf_op | source)
XLA Modules:
  0.0 76.1 jit_solution(14482491908795377601)
XLA Ops:
  0.0 74.2 %shard_map.109 = bf16[32,16,512]{2,1,0:T(8,128)(2,1)} custom-call(bf16[32,16,512]{2,1,0:T(8,128)(2,1)} %pair.1, bf16[2,4,32,128]{3,2,1,0:T(8,128)(2,1)} %bitcast.4, bf16[2,32,128]{2,1,0:T(8,128)(2,1)} %bitcast.5, bf16[2,128,128]{2,1,0:T(8,128)(2,1)} %wout_hbm.1, f32[2,128]{1,0:T(2,128)} %pgain_hbm.1, f32[2,128]{1,0:T(2,128)} %pbias_hbm.1, ...), custom_call_target="tpu_custom_call" | custom-call | tf_op jit(solution)/shard_map/pallas_call | solution.py:321
  74.2 1.9 %copy.13 = bf16[32,16,512]{2,1,0:T(8,128)(2,1)} copy(bf16[32,16,512]{2,1,0:T(8,128)(2,1)} %shard_map.109) | data formatting | bytes 1048576

commit v7 on v6

--- a/solution.py
+++ b/solution.py
@@ -27,6 +27,10 @@
     return (v - center) * lax.rsqrt(spread + 1e-05) * gain + offset
 
 
+def twice(v):
+    return jnp.concatenate([v, v], axis=1)
+
+
 def columns(row):
     return jnp.broadcast_to(row, (128, 128)).T
 
@@ -38,7 +42,7 @@
 def kernel(
     pair, win, wgate, wout_hbm, pgain_hbm, pbias_hbm, hgain_hbm, hbias_hbm, cgain_hbm, mask_hbm, chain_hbm, out,
     wout, pgain, pbias, hgain, hbias, cgain, mask, chain,
-    pbuf, win_all, wgate_all, wout_t, mysmall, small_all, par, edge, turn, turn_lr,
+    pbuf, win_all, wgate_all, wout_t, mysmall, small_all, par, edge, turn, turn_lr, turn_out,
     cur, normed, gate, stage, lr, tbuf, tri, obuf,
     p_send, p_recv, p_own, w_send, w_recv, w_own, lr_send, first_recv, second_recv, t_send, t_recv, o_send, o_recv, o_own, f_own, ready,
 ):
@@ -157,18 +161,6 @@
     edge[0] = own_rows(0) * mask[pl.ds(c, 1), :].astype(F32)
     edge[1] = jnp.where(own_rows(1) != chain[pl.ds(c, 1), :].astype(F32), 1.0, 0.0)
 
-    kept.wait()
-    for cp in moved:
-        cp.wait()
-    turn[...] = pbuf[...].astype(F32).reshape(2048, 128)
-
-    @pl.loop(0, 16, unroll=4)
-    def _(i):
-        v = turn[pl.ds(i, 128, stride=16), :]
-        at = aligned(i, 128)
-        cur[:, at] = v
-        normed[:, at] = norm(v, par[0], par[2]).astype(BF16)
-
     for cp in kept_w[:2] + moved_sm:
         cp.wait()
     lanes = lax.broadcasted_iota(jnp.int32, (8, 128), 1)
@@ -180,7 +172,42 @@
     for cp in moved_w0:
         cp.wait()
 
+    def of_group(u, q):
+        g = lax.rem(group + q, 4)
+        rows_g = aligned(g, 32)
+        return g, rows_g, win_all[u, :, rows_g, :].reshape(128, 128), par[8 + u, rows_g, :]
+
+    def project(weight, cross, b, columns_b):
+        proj = dot(weight, columns_b)
+        left = sigmoid(proj[0:32]) * proj[32:64]
+        right = sigmoid(proj[64:96]) * proj[96:128]
+        for k in range(2):
+            i = 2 * b + k
+            factor = edge[0, pl.ds(i, 1), :] * jnp.where(edge[1, pl.ds(i, 1), :] > 0.5, cross, 1.0)
+            half = slice(128 * k, 128 * (k + 1))
+            turn_lr[pl.ds(i, 32, stride=16), :] = factor * left[:, half]
+            turn_lr[pl.ds(512 + i, 32, stride=16), :] = factor * right[:, half]
+
+    kept.wait()
+    for cp in moved:
+        cp.wait()
+    turn[...] = pbuf[...].astype(F32).reshape(2048, 128)
+    _, _, weight, cross = of_group(0, 0)
+
+    @pl.loop(0, 8, unroll=8)
+    def _(b, weight=weight, cross=cross):
+        at = aligned(b, 256)
+        v = jnp.concatenate([turn[pl.ds(2 * b + k, 128, stride=16), :] for k in range(2)], axis=1)
+        cur[:, at] = v
+        fresh = norm(v, twice(par[0]), twice(par[2])).astype(BF16)
+        normed[:, at] = fresh
+        project(weight, cross, b, fresh)
+
     later = []
+
+    def tri_columns(u, b):
+        v = jnp.concatenate([turn[pl.ds(2 * b + k, 128, stride=16), :] for k in range(2)], axis=1)
+        return norm(v, twice(par[4 + u]), twice(par[6 + u])).astype(BF16)
 
     def landing(u, k):
         row = spot_row if (u, k) == (0, 0) else r
@@ -200,22 +227,12 @@
     for u in range(2):
         first, second = (1, 0) if u == 0 else (0, 1)
         for q in range(4):
-            g = lax.rem(group + q, 4)
-            rows_g = aligned(g, 32)
-            weight = win_all[u, :, rows_g, :].reshape(128, 128)
-            cross = par[8 + u, rows_g, :]
-
-            @pl.loop(0, 8, unroll=8)
-            def _(b, u=u, weight=weight, cross=cross):
-                proj = dot(weight, normed[:, aligned(b, 256)])
-                left = sigmoid(proj[0:32]) * proj[32:64]
-                right = sigmoid(proj[64:96]) * proj[96:128]
-                for k in range(2):
-                    i = 2 * b + k
-                    factor = edge[0, pl.ds(i, 1), :] * jnp.where(edge[1, pl.ds(i, 1), :] > 0.5, cross, 1.0)
-                    half = slice(128 * k, 128 * (k + 1))
-                    turn_lr[pl.ds(i, 32, stride=16), :] = factor * left[:, half]
-                    turn_lr[pl.ds(512 + i, 32, stride=16), :] = factor * right[:, half]
+            g, rows_g, weight, cross = of_group(u, q)
+            if q > 0:
+
+                @pl.loop(0, 8, unroll=8)
+                def _(b, weight=weight, cross=cross):
+                    project(weight, cross, b, normed[:, aligned(b, 256)])
 
             for k in range(2):
                 stage[u, rows_g, k] = turn_lr[512 * k : 512 * (k + 1), :].astype(BF16).reshape(32, 16, 128)
@@ -285,27 +302,44 @@
         )
         turn[...] = tri[u].astype(F32).reshape(2048, 128)
 
+        if u == 0:
+            _, _, weight, cross = of_group(1, 0)
+
+            @pl.loop(0, 8, unroll=8)
+            def _(b, weight=weight, cross=cross):
+                at = aligned(b, 256)
+                update = dot(wout_t[0], tri_columns(0, b))
+                new = (cur[:, at] + gate[:, at] * update).astype(BF16).astype(F32)
+                cur[:, at] = new
+                fresh = norm(new, twice(par[1]), twice(par[3])).astype(BF16)
+                normed[:, at] = fresh
+                project(weight, cross, b, fresh)
+
+    here = out.at[:, :, aligned(c, 128)]
+    last = []
+    for turned_half in range(2):
+        half = lax.rem(lax.div(c, 2) + 1 + turned_half, 2)
+        rows_h = aligned(half, 64)
+
         @pl.loop(0, 8, unroll=8)
-        def _(b, u=u):
+        def _(b, first_half=turned_half == 0, half=half, rows_h=rows_h):
             at = aligned(b, 256)
-            halves = [
-                norm(turn[pl.ds(2 * b + k, 128, stride=16), :], par[4 + u], par[6 + u]).astype(BF16) for k in range(2)
-            ]
-            update = dot(wout_t[u], jnp.concatenate(halves, axis=1))
-            new = (cur[:, at] + gate[:, at] * update).astype(BF16).astype(F32)
-            if u == 0:
-                cur[:, at] = new
-                for k in range(2):
-                    at2 = aligned(2 * b + k, 128)
-                    half = new[:, 128 * k : 128 * (k + 1)]
-                    normed[:, at2] = norm(half, par[1], par[3]).astype(BF16)
-            else:
-                for k in range(2):
-                    turn[pl.ds(2 * b + k, 128, stride=16), :] = new[:, 128 * k : 128 * (k + 1)]
-
-    obuf[...] = turn[...].astype(BF16).reshape(128, 16, 128)
-    here = out.at[:, :, aligned(c, 128)]
-    last = spread(0, lambda c2: obuf.at[aligned(c2, 32)], here, o_send, o_recv, c_peers)
+            if first_half:
+                normed[:, at] = tri_columns(1, b)
+            update = dot(wout_t[1, rows_h, :], normed[:, at])
+            new = cur[rows_h, at] + gate[rows_h, at] * update
+            for k in range(2):
+                turn_out[pl.ds(2 * b + k, 64, stride=16), :] = new[:, 128 * k : 128 * (k + 1)]
+
+        obuf[rows_h] = turn_out[...].astype(BF16).reshape(64, 16, 128)
+        for s in range(2) if turned_half == 0 else (2,):
+            c2 = c_peers[s][1]
+            cp = pltpu.make_async_remote_copy(
+                src_ref=obuf.at[aligned(c2, 32)], dst_ref=here, send_sem=o_send.at[0, s], recv_sem=o_recv.at[0, s],
+                device_id=c_peers[s], device_id_type=MESH,
+            )
+            cp.start()
+            last.append(cp)
     own(0, obuf.at[rows_c], here, o_own).wait()
     for cp in last:
         cp.wait()
@@ -342,6 +376,7 @@
             pltpu.VMEM((2, 16, 128), F32),
             pltpu.VMEM((2048, 128), F32),
             pltpu.VMEM((1024, 128), F32),
+            pltpu.VMEM((1024, 128), F32),
             pltpu.VMEM((128, 2048), F32),
             pltpu.VMEM((128, 2048), BF16),
             pltpu.VMEM((128, 2048), F32),

time: 76.3 us -> 75 us (0.983)
  Pallas kernels: 74.2 us -> 73 us
    pallas_call x1, Pallas kernels: 74.2 us -> 73 us  [per_device(): pl.pallas_call(kernel, out_shape=jax.ShapeDtypeStruct((32, 16, 512), BF16...]
where the time goes in v7:
time: 75 us; the launch traced here: 74.9 us
  Pallas kernels  73 us (97%)
  local copies, waits for them, and re-layouts  1.87 us (2%)
    pallas_call x1, Pallas kernels, per_device(): pl.pallas_call(kernel, out_shape=jax.ShapeDtypeStruct((32, 16, 512), BF16...  73 us
    unnamed x1, local copies, waits for them, and re-layouts  1.87 us

profile of v7, /device:TPU:1, one launch (start us, length us, event | category | flops | bytes accessed | tf_op | source)
XLA Modules:
  0.0 74.9 jit_solution(13403702670254759557)
XLA Ops:
  0.0 73.0 %shard_map.109 = bf16[32,16,512]{2,1,0:T(8,128)(2,1)} custom-call(bf16[32,16,512]{2,1,0:T(8,128)(2,1)} %pair.1, bf16[2,4,32,128]{3,2,1,0:T(8,128)(2,1)} %bitcast.4, bf16[2,32,128]{2,1,0:T(8,128)(2,1)} %bitcast.5, bf16[2,128,128]{2,1,0:T(8,128)(2,1)} %wout_hbm.1, f32[2,128]{1,0:T(2,128)} %pgain_hbm.1, f32[2,128]{1,0:T(2,128)} %pbias_hbm.1, ...), custom_call_target="tpu_custom_call" | custom-call | tf_op jit(solution)/shard_map/pallas_call | solution.py:355
  73.0 1.9 %copy.13 = bf16[32,16,512]{2,1,0:T(8,128)(2,1)} copy(bf16[32,16,512]{2,1,0:T(8,128)(2,1)} %shard_map.109) | data formatting | bytes 1048576

commit v8 on v7

--- a/solution.py
+++ b/solution.py
@@ -211,7 +211,7 @@
 
     def landing(u, k):
         row = spot_row if (u, k) == (0, 0) else r
-        return lr.at[u, k, aligned(row, 16), aligned(c, 128)]
+        return lr.at[u, k, c, aligned(row, 16)]
 
     def send_lr(u, k, sem, h2, r2, c2):
         pltpu.make_async_remote_copy(
@@ -263,44 +263,54 @@
         arrived(lr.at[u, first], lr.at[u, first], lr_send.at[u], first_recv.at[u]).wait_recv()
         later.append(arrived(stage.at[u, pl.ds(0, 127)], stage.at[u, pl.ds(0, 127)], lr_send.at[u], first_recv.at[u]))
 
-        def send_t(_, r2, c2, u=u):
+        def send_t(sem, _, r2, c2, u=u):
             row = hidden_row(r2) if u == 0 else r2
             pltpu.make_async_remote_copy(
-                src_ref=tbuf.at[u, aligned(row, 16), aligned(c2, 128)], dst_ref=tri.at[u, mine],
-                send_sem=t_send.at[u], recv_sem=t_recv.at[u], device_id=(r2, c2), device_id_type=MESH,
+                src_ref=tbuf.at[u, c2, aligned(row, 16)], dst_ref=tri.at[u, mine],
+                send_sem=t_send.at[u], recv_sem=sem, device_id=(r2, c2), device_id_type=MESH,
             ).start()
 
         for q in range(4):
             if u == 0:
                 g = lax.rem(group + 4 - q, 4)
-                part = lr.at[0, 0, aligned(g, 128)]
+                rows_g = aligned(g, 128)
+                part = lr.at[0, 0, :, rows_g]
                 arrived(part, part, lr_send.at[u], second_recv.at[u, q]).wait_recv()
-                tbuf[0, aligned(g, 128), :] = dot(part[...], lr[0, 1], ((1,), (1,))).astype(BF16)
-                each(g, send_t, 1 if q == 0 else 0)
+                left = jnp.concatenate([lr[0, 0, k, rows_g, :] for k in range(4)], axis=1)
+                right = jnp.concatenate([lr[0, 1, k] for k in range(4)], axis=1)
+                product = dot(left, right, ((1,), (1,))).astype(BF16)
+                for k in range(4):
+                    tbuf[0, k, rows_g, :] = product[:, 128 * k : 128 * (k + 1)]
+                each(g, functools.partial(send_t, t_recv.at[0, q]), 1 if q == 0 else 0)
             else:
                 c2 = lax.rem(c + 4 - q, 4)
-                part = lr.at[1, 1, :, aligned(c2, 128)]
+                part = lr.at[1, 1, c2]
                 arrived(part, part, lr_send.at[u], second_recv.at[u, q]).wait_recv()
-                tbuf[1, :, aligned(c2, 128)] = dot(lr[1, 0], part[...], ((0,), (0,))).astype(BF16)
+                left = jnp.concatenate([lr[1, 0, k] for k in range(4)], axis=1)
+                tbuf[1, c2] = dot(left, part[...], ((0,), (0,))).astype(BF16)
 
                 @pl.loop(1 if q == 0 else 0, 32)
                 def _(j, c2=c2, send_t=send_t):
-                    send_t(None, lax.rem(r + j, 32), c2)
+                    send_t(t_recv.at[1, 0], None, lax.rem(r + j, 32), c2)
 
         pltpu.make_async_copy(
-            tbuf.at[u, aligned(spot_row if u == 0 else r, 16), aligned(c, 128)], tri.at[u, mine], t_recv.at[u]
+            tbuf.at[u, c, aligned(spot_row if u == 0 else r, 16)], tri.at[u, mine], t_recv.at[u, 0]
         ).start()
-        pltpu.make_async_remote_copy(
-            src_ref=tri.at[u], dst_ref=tri.at[u], send_sem=t_send.at[u], recv_sem=t_recv.at[u],
-            device_id=(r, peers[0]), device_id_type=MESH,
-        ).wait_recv()
         later.append(
             pltpu.make_async_remote_copy(
                 src_ref=tri.at[u, pl.ds(0, 127)], dst_ref=tri.at[u, pl.ds(0, 127)], send_sem=t_send.at[u],
-                recv_sem=t_recv.at[u], device_id=(r, peers[0]), device_id_type=MESH,
+                recv_sem=t_recv.at[u, 0], device_id=(r, peers[0]), device_id_type=MESH,
             )
         )
-        turn[...] = tri[u].astype(F32).reshape(2048, 128)
+        if u == 0:
+            for q in range(4):
+                g = lax.rem(group + q, 4)
+                rows_g = tri.at[0, aligned(g, 32)]
+                arrived(rows_g, rows_g, t_send.at[0], t_recv.at[0, q]).wait_recv()
+                turn[aligned(g, 512), :] = rows_g[...].astype(F32).reshape(512, 128)
+        else:
+            arrived(tri.at[1], tri.at[1], t_send.at[1], t_recv.at[1, 0]).wait_recv()
+            turn[...] = tri[1].astype(F32).reshape(2048, 128)
 
         if u == 0:
             _, _, weight, cross = of_group(1, 0)
@@ -381,13 +391,13 @@
             pltpu.VMEM((128, 2048), BF16),
             pltpu.VMEM((128, 2048), F32),
             pltpu.VMEM((2, 128, 2, 16, 128), BF16),
-            pltpu.VMEM((2, 2, 512, 512), BF16),
-            pltpu.VMEM((2, 512, 512), BF16),
+            pltpu.VMEM((2, 2, 4, 512, 128), BF16),
+            pltpu.VMEM((2, 4, 512, 128), BF16),
             pltpu.VMEM((2, 128, 16, 128), BF16),
             pltpu.VMEM((128, 16, 128), BF16),
             dma((1, 3)), dma((1, 3)), dma((1,)),
             dma((4, 3)), dma((4, 3)), dma((4,)),
-            dma((2,)), dma((2,)), dma((2, 4)), dma((2,)), dma((2,)),
+            dma((2,)), dma((2,)), dma((2, 4)), dma((2,)), dma((2, 4)),
             dma((1, 3)), dma((1, 3)), dma((1,)), dma((8,)),
             pltpu.SemaphoreType.REGULAR((3,)),
         ],

time: 75 us -> 75.3 us (level)
  no operation moved by 1% of the time
where the time goes in v8:
time: 75.3 us; the launch traced here: 75.1 us
  Pallas kernels  73.2 us (97%)
  local copies, waits for them, and re-layouts  1.87 us (2%)
    pallas_call x1, Pallas kernels, per_device(): pl.pallas_call(kernel, out_shape=jax.ShapeDtypeStruct((32, 16, 512), BF16...  73.2 us
    unnamed x1, local copies, waits for them, and re-layouts  1.87 us

profile of v8, /device:TPU:1, one launch (start us, length us, event | category | flops | bytes accessed | tf_op | source)
XLA Modules:
  0.0 75.1 jit_solution(17594659606001740862)
XLA Ops:
  0.0 73.2 %shard_map.109 = bf16[32,16,512]{2,1,0:T(8,128)(2,1)} custom-call(bf16[32,16,512]{2,1,0:T(8,128)(2,1)} %pair.1, bf16[2,4,32,128]{3,2,1,0:T(8,128)(2,1)} %bitcast.4, bf16[2,32,128]{2,1,0:T(8,128)(2,1)} %bitcast.5, bf16[2,128,128]{2,1,0:T(8,128)(2,1)} %wout_hbm.1, f32[2,128]{1,0:T(2,128)} %pgain_hbm.1, f32[2,128]{1,0:T(2,128)} %pbias_hbm.1, ...), custom_call_target="tpu_custom_call" | custom-call | tf_op jit(solution)/shard_map/pallas_call | solution.py:365
  73.2 1.9 %copy.13 = bf16[32,16,512]{2,1,0:T(8,128)(2,1)} copy(bf16[32,16,512]{2,1,0:T(8,128)(2,1)} %shard_map.109) | data formatting | bytes 1048576
